TPU v7x, 512 devices: a whole 4x8x8 slice. The times are simulated.
512 devices in a mesh: gx: 8 (over x, core), gy: 8 (over z), gz: 8 (over y).
Axes of the slice: x: 4, y: 8, z: 8, core: 2. Of those that a mesh axis runs over, the one named last changes fastest.
Arguments:
- velocity: float32 [3, 128, 128, 1024], P(None, 'gx', 'gy', 'gz'), may hold values from -6 to 6
- input_weight: bfloat16 [32, 9], replicated, may hold values from -2 to 2
- input_bias: float32 [32], replicated, may hold values from -3 to 3
- hidden_weight: bfloat16 [32, 32], replicated, may hold values from -1 to 1
- hidden_bias: float32 [32], replicated, may hold values from -3 to 3
- output_weight: bfloat16 [32], replicated, may hold values from -1 to 1
Outputs:
- velocity_new: float32 [3, 128, 128, 1024], P(None, 'gx', 'gy', 'gz')
- pressure: float32 [128, 128, 1024], P('gx', 'gy', 'gz')
All inputs are finite; a program needn't handle non-finite values.
Results may differ from a plain program's by a relative error of at most 0.00039.
Values sent between devices are 32-bit elements; how exact they have to be, the bound alone decides.
A program may use at most 64 MiB of HBM per device.

v0:
```python
import jax
import jax.numpy as jnp
from jax import lax
from jax.sharding import PartitionSpec as P

LEVELS = 4


time_step = 0.1
closure_gain = 0.5
jacobi_weight = 0.8


def with_halo(array, sides, width):
    for axis, dim in sides:
        size, length = (lax.axis_size(axis), array.shape[dim])
        up = [(i, (i + 1) % size) for i in range(size)]
        down = [(j, i) for i, j in up]
        last = lax.slice_in_dim(array, length - width, length, axis=dim)
        initial = lax.slice_in_dim(array, 0, width, axis=dim)
        before = lax.ppermute(last, axis, up)
        after = lax.ppermute(initial, axis, down)
        array = jnp.concatenate([before, array, after], axis=dim)
    return array


def leading(padded):
    return (slice(None),) * (padded.ndim - 3)


def shifted(padded, direction, offset):
    window = [slice(1, -1), slice(1, -1), slice(1, -1)]
    length = padded.shape[padded.ndim - 3 + direction]
    window[direction] = slice(1 + offset, length - 1 + offset)
    return padded[leading(padded) + tuple(window)]


def interior(padded):
    return padded[leading(padded) + (slice(1, -1), slice(1, -1), slice(1, -1))]


def laplace(padded, grid_level):
    summed = shifted(padded, 0, 1) + shifted(padded, 0, -1)
    summed = summed + shifted(padded, 1, 1) + shifted(padded, 1, -1)
    summed = summed + shifted(padded, 2, 1) + shifted(padded, 2, -1)
    return (summed - 6.0 * interior(padded)) * 0.25**grid_level


def restrict(fine):
    shaped = fine.reshape(fine.shape[0] // 2, 2, fine.shape[1] // 2, 2, fine.shape[2] // 2, 2)
    return 0.125 * shaped.sum(axis=(1, 3, 5))


def prolong(coarse):
    return jnp.repeat(jnp.repeat(jnp.repeat(coarse, 2, 0), 2, 1), 2, 2)


def gradient_features(padded):
    gradient = [
        [
            0.5
            * (shifted(padded[component], direction, 1) - shifted(padded[component], direction, -1))
            for direction in range(3)
        ]
        for component in range(3)
    ]
    listing = [
        gradient[0][0],
        gradient[1][1],
        gradient[2][2],
        0.5 * (gradient[0][1] + gradient[1][0]),
        0.5 * (gradient[0][2] + gradient[2][0]),
        0.5 * (gradient[1][2] + gradient[2][1]),
        0.5 * (gradient[0][1] - gradient[1][0]),
        0.5 * (gradient[0][2] - gradient[2][0]),
        0.5 * (gradient[1][2] - gradient[2][1]),
    ]
    region = listing[0].shape
    stacked = jnp.stack([entry.reshape(region[0] // 2, -1) for entry in listing], axis=1)
    return (stacked.astype(jnp.bfloat16), region)


def closure(features, region, input_weight, input_bias, hidden_weight, hidden_bias, output_weight):

    def apply_block(block_cells):
        hidden = jnp.tanh(
            jnp.dot(input_weight, block_cells, preferred_element_type=jnp.float32)
            + input_bias[:, None]
        ).astype(jnp.bfloat16)
        second = jnp.tanh(
            jnp.dot(hidden_weight, hidden, preferred_element_type=jnp.float32)
            + hidden_bias[:, None]
        ).astype(jnp.bfloat16)
        return closure_gain * jax.nn.softplus(
            jnp.dot(output_weight, second, preferred_element_type=jnp.float32)
        )

    return lax.map(apply_block, features).reshape(region)


def tendency(padded_velocity, padded_viscosity):
    viscosity_mid = interior(padded_viscosity)
    provisional_list = []
    for component in range(3):
        center = interior(padded_velocity[component])
        advect = 0.0
        diffuse = 0.0
        for direction in range(3):
            product = padded_velocity[direction] * padded_velocity[component]
            advect = advect + 0.5 * (
                shifted(product, direction, 1) - shifted(product, direction, -1)
            )
            upward = (
                0.5
                * (viscosity_mid + shifted(padded_viscosity, direction, 1))
                * (shifted(padded_velocity[component], direction, 1) - center)
            )
            downward = (
                0.5
                * (viscosity_mid + shifted(padded_viscosity, direction, -1))
                * (center - shifted(padded_velocity[component], direction, -1))
            )
            diffuse = diffuse + (upward - downward)
        provisional_list.append(center + time_step * (diffuse - advect))
    return jnp.stack(provisional_list)


def pressure_halo(stacked, width_cells):
    return with_halo(stacked, (("gx", 1), ("gy", 2), ("gz", 3)), width_cells)


def single_sweep(iterate, source, grid_level, factor):
    padded = pressure_halo(iterate[None], 1)[0]
    return iterate - factor * (source - laplace(padded, grid_level))


def double_sweep(iterate, source, grid_level, factor):
    iterate = single_sweep(iterate, source, grid_level, factor)
    return single_sweep(iterate, source, grid_level, factor)


def multigrid_cycle(source, grid_level):
    factor = jacobi_weight * 4.0**grid_level / 6.0
    if grid_level == LEVELS - 1:
        iterate = -(factor * source)
        iterate = single_sweep(iterate, source, grid_level, factor)
        return double_sweep(iterate, source, grid_level, factor)
    iterate = -(factor * source)
    iterate = single_sweep(iterate, source, grid_level, factor)
    padded = pressure_halo(iterate[None], 1)[0]
    residual = source - laplace(padded, grid_level)
    correction = multigrid_cycle(restrict(residual), grid_level + 1)
    iterate = iterate + prolong(correction)
    return double_sweep(iterate, source, grid_level, factor)


def body(velocity, input_weight, input_bias, hidden_weight, hidden_bias, output_weight):
    padded_velocity = with_halo(velocity, (("gx", 1), ("gy", 2), ("gz", 3)), 1)
    features, region = gradient_features(padded_velocity)
    viscosity = closure(
        features, region, input_weight, input_bias, hidden_weight, hidden_bias, output_weight
    )
    padded_viscosity = with_halo(viscosity, (("gx", 0), ("gy", 1), ("gz", 2)), 1)
    provisional = tendency(padded_velocity, padded_viscosity)
    padded_star = with_halo(provisional, (("gx", 1), ("gy", 2), ("gz", 3)), 1)
    divergence = 0.0
    for direction in range(3):
        divergence = divergence + 0.5 * (
            shifted(padded_star[direction], direction, 1)
            - shifted(padded_star[direction], direction, -1)
        )
    pressure = multigrid_cycle(divergence, 0)
    padded_pressure = pressure_halo(pressure[None], 1)[0]
    velocity_new = jnp.stack(
        [
            provisional[direction]
            - 0.5
            * (shifted(padded_pressure, direction, 1) - shifted(padded_pressure, direction, -1))
            for direction in range(3)
        ]
    )
    return (velocity_new, pressure)


def solution(mesh):
    return jax.shard_map(
        body,
        mesh=mesh,
        in_specs=(P(None, "gx", "gy", "gz"), P(), P(), P(), P(), P()),
        out_specs=(P(None, "gx", "gy", "gz"), P("gx", "gy", "gz")),
        check_vma=False,
    )
```

profile of v0, /device:TPU:1, one launch (start us, length us, event | category | flops | bytes accessed | tf_op | source)
XLA Modules:
  0.0 496.7 jit_solution(7356898099685791698)
XLA Ops:
  4.0 4.3 collective-permute-start.1
  12.0 7.9 %collective-permute-start.3 = (f32[3,18,1,128]{3,2,1,0:T(1,128)S(1)}, f32[3,18,1,128]{3,2,1,0:T(1,128)S(1)}, u32[]{:S(2)}, u32[]{:S(2)}) collective-permute-start(f32[3,18,1,128]{3,2,1,0:T(1,128)S(1)} %get-tuple-element.113), channel_id=1, source_target_pairs={{8,0},{16,8},{24,16},{32,24},{40,32},{48,40},{56,48},{0,56},{9,1},... | collective-permute-start | bytes 82952 | tf_op jit(solution)/shard_map/ppermute | solution.py:22
  34.1 15.7 %while.10 = (s32[]{:T(128)}, f32[8,4096]{1,0:T(8,128)S(1)}, bf16[8,9,4096]{2,1,0:T(8,128)(2,1)}, bf16[32,9]{0,1:T(8,128)(2,1)S(1)}, f32[32]{0:T(128)S(1)}, /*ind...) while((s32[]{:T(128)}, f32[8,4096]{1,0:T(8,128)S(1)}, ...), condition=%wide.region_1.2_spmd, body=%wide.region_0.1_spmd.sunk | while | flops 11563010 | bytes 740341 | solution.py:98
  57.9 5.1 %collective-permute-start.8 = (f32[18,1,128]{2,1,0:T(1,128)S(1)}, f32[18,1,128]{2,1,0:T(1,128)S(1)}, u32[]{:S(2)}, u32[]{:S(2)}) collective-permute-start(f32[18,1,128]{2,1,0:T(1,128)S(1)} %get-tuple-element.141), channel_id=1, source_target_pairs={{8,0},{16,8},{24,16},{32,24},{40,32},{48,40},{56,48},{0,56},{9,1},... | collective-permute-start | bytes 27656 | tf_op jit(solution)/shard_map/ppermute | solution.py:22
  92.8 4.8 collective-permute-start.16
  153.9 9.7 %reshape.85 = f32[8,2,8,2,64,2]{5,4,3,2,1,0:T(8,128)} reshape(f32[16,16,128]{2,1,0:T(8,128)S(1)} %fusion.30) | data formatting | bytes 262144 | tf_op jit(solution)/shard_map/reshape | solution.py:50
  163.6 4.0 reduce_sum.27
  167.7 4.1 collective-permute-start.30
  231.2 4.2 collective-permute-start.47
  245.9 3.9 collective-permute-start.51
  253.6 3.9 collective-permute-start.53
  260.0 4.6 collective-permute-start.55
  268.2 3.9 collective-permute-start.57
  281.3 5.5 %collective-permute-start.61 = (f32[1,1,2,16]{3,2,1,0:T(2,128)S(1)}, f32[1,1,2,16]{3,2,1,0:T(2,128)S(1)}, u32[]{:S(2)}, u32[]{:S(2)}) collective-permute-start(f32[1,1,2,16]{3,2,1,0:T(2,128)S(1)} %get-tuple-element.217), channel_id=1, source_target_pairs={{64,0},{128,64},{192,128},{256,192},{320,256},{384,320},{448,384},... | collective-permute-start | bytes 392 | tf_op jit(solution)/shard_map/ppermute | solution.py:22
  304.1 5.7 %collective-permute-start.67 = (f32[1,1,2,16]{3,2,1,0:T(2,128)S(1)}, f32[1,1,2,16]{3,2,1,0:T(2,128)S(1)}, u32[]{:S(2)}, u32[]{:S(2)}) collective-permute-start(f32[1,1,2,16]{3,2,1,0:T(2,128)S(1)} %get-tuple-element.215), channel_id=1, source_target_pairs={{64,0},{128,64},{192,128},{256,192},{320,256},{384,320},{448,384},... | collective-permute-start | bytes 392 | tf_op jit(solution)/shard_map/ppermute | solution.py:22
  327.2 6.3 %collective-permute-start.73 = (f32[1,1,4,32]{3,2,1,0:T(4,128)S(1)}, f32[1,1,4,32]{3,2,1,0:T(4,128)S(1)}, u32[]{:S(2)}, u32[]{:S(2)}) collective-permute-start(f32[1,1,4,32]{3,2,1,0:T(4,128)S(1)} %get-tuple-element.197), channel_id=1, source_target_pairs={{64,0},{128,64},{192,128},{256,192},{320,256},{384,320},{448,384},... | collective-permute-start | bytes 1544 | tf_op jit(solution)/shard_map/ppermute | solution.py:22
  349.6 6.3 %collective-permute-start.79 = (f32[1,1,4,32]{3,2,1,0:T(4,128)S(1)}, f32[1,1,4,32]{3,2,1,0:T(4,128)S(1)}, u32[]{:S(2)}, u32[]{:S(2)}) collective-permute-start(f32[1,1,4,32]{3,2,1,0:T(4,128)S(1)} %get-tuple-element.195), channel_id=1, source_target_pairs={{64,0},{128,64},{192,128},{256,192},{320,256},{384,320},{448,384},... | collective-permute-start | bytes 1544 | tf_op jit(solution)/shard_map/ppermute | solution.py:22
  367.1 3.9 collective-permute-start.83
  372.6 6.0 %collective-permute-start.85 = (f32[1,1,8,64]{3,2,1,0:T(8,128)S(1)}, f32[1,1,8,64]{3,2,1,0:T(8,128)S(1)}, u32[]{:S(2)}, u32[]{:S(2)}) collective-permute-start(f32[1,1,8,64]{3,2,1,0:T(8,128)S(1)} %get-tuple-element.173), channel_id=1, source_target_pairs={{64,0},{128,64},{192,128},{256,192},{320,256},{384,320},{448,384},... | collective-permute-start | bytes 6152 | tf_op jit(solution)/shard_map/ppermute | solution.py:22
  395.6 6.0 %collective-permute-start.91 = (f32[1,1,8,64]{3,2,1,0:T(8,128)S(1)}, f32[1,1,8,64]{3,2,1,0:T(8,128)S(1)}, u32[]{:S(2)}, u32[]{:S(2)}) collective-permute-start(f32[1,1,8,64]{3,2,1,0:T(8,128)S(1)} %get-tuple-element.171), channel_id=1, source_target_pairs={{64,0},{128,64},{192,128},{256,192},{320,256},{384,320},{448,384},... | collective-permute-start | bytes 6152 | tf_op jit(solution)/shard_map/ppermute | solution.py:22
  412.8 3.9 collective-permute-start.95
  419.6 5.7 %collective-permute-start.97 = (f32[1,1,16,128]{3,2,1,0:T(8,128)S(1)}, f32[1,1,16,128]{3,2,1,0:T(8,128)S(1)}, u32[]{:S(2)}, u32[]{:S(2)}) collective-permute-start(f32[1,1,16,128]{3,2,1,0:T(8,128)S(1)} %get-tuple-element.147), channel_id=1, source_target_pairs={{64,0},{128,64},{192,128},{256,192},{320,256},{384,320},{448,384},... | collective-permute-start | bytes 24584 | tf_op jit(solution)/shard_map/ppermute | solution.py:22
  436.7 4.1 collective-permute-start.101
  453.8 3.9 collective-permute-start.105
  (452 shorter events, 375.8 us)
Async XLA Ops:
  1.4 7.6 %collective-permute-start = (f32[3,1,16,128]{3,2,1,0:T(8,128)S(1)}, f32[3,1,16,128]{3,2,1,0:T(8,128)S(1)}, u32[]{:S(2)}, u32[]{:S(2)}) collective-permute-start(f32[3,1,16,128]{3,2,1,0:T(8,128)S(1)} %get-tuple-element.117), channel_id=1, source_target_pairs={{0,64},{64,128},{128,192},{192,256},{256,320},{320,384},{384,448},... | collective-permute-start | bytes 73736 | tf_op jit(solution)/shard_map/ppermute | solution.py:21
  10.1 9.8 %collective-permute-start.2 = (f32[3,18,1,128]{3,2,1,0:T(1,128)S(1)}, f32[3,18,1,128]{3,2,1,0:T(1,128)S(1)}, u32[]{:S(2)}, u32[]{:S(2)}) collective-permute-start(f32[3,18,1,128]{3,2,1,0:T(1,128)S(1)} %get-tuple-element.112), channel_id=1, source_target_pairs={{0,8},{8,16},{16,24},{24,32},{32,40},{40,48},{48,56},{56,0},{1,9},... | collective-permute-start | bytes 82952 | tf_op jit(solution)/shard_map/ppermute | solution.py:21
  12.0 8.9 %collective-permute-start.3 = (f32[3,18,1,128]{3,2,1,0:T(1,128)S(1)}, f32[3,18,1,128]{3,2,1,0:T(1,128)S(1)}, u32[]{:S(2)}, u32[]{:S(2)}) collective-permute-start(f32[3,18,1,128]{3,2,1,0:T(1,128)S(1)} %get-tuple-element.113), channel_id=1, source_target_pairs={{8,0},{16,8},{24,16},{32,24},{40,32},{48,40},{56,48},{0,56},{9,1},... | collective-permute-start | bytes 82952 | tf_op jit(solution)/shard_map/ppermute | solution.py:22
  21.6 7.5 %collective-permute-start.4 = (f32[3,18,18,1]{2,3,1,0:T(1,128)S(1)}, f32[3,18,18,1]{2,3,1,0:T(1,128)S(1)}, u32[]{:S(2)}, u32[]{:S(2)}) collective-permute-start(f32[3,18,18,1]{2,3,1,0:T(1,128)S(1)} %copy.36), channel_id=1, source_target_pairs={{0,1},{1,2},{2,3},{3,4},{4,5},{5,6},{6,7},{7,0},{8,9},{9,10},{10,1... | collective-permute-start | bytes 11672 | tf_op jit(solution)/shard_map/ppermute | solution.py:21
  56.0 7.1 %collective-permute-start.9 = (f32[18,1,128]{2,1,0:T(1,128)S(1)}, f32[18,1,128]{2,1,0:T(1,128)S(1)}, u32[]{:S(2)}, u32[]{:S(2)}) collective-permute-start(f32[18,1,128]{2,1,0:T(1,128)S(1)} %get-tuple-element.140), channel_id=1, source_target_pairs={{0,8},{8,16},{16,24},{24,32},{32,40},{40,48},{48,56},{56,0},{1,9},... | collective-permute-start | bytes 27656 | tf_op jit(solution)/shard_map/ppermute | solution.py:21
  64.0 8.1 %collective-permute-start.11 = (f32[18,18,1]{2,1,0:T(8,128)S(1)}, f32[18,18,1]{2,1,0:T(8,128)S(1)}, u32[]{:S(2)}, u32[]{:S(2)}) collective-permute-start(f32[18,18,1]{2,1,0:T(8,128)S(1)} %get-tuple-element.128), channel_id=1, source_target_pairs={{0,1},{1,2},{2,3},{3,4},{4,5},{5,6},{6,7},{7,0},{8,9},{9,10},{10,1... | collective-permute-start | bytes 3896 | tf_op jit(solution)/shard_map/ppermute | solution.py:21
  67.3 7.6 %collective-permute-start.10 = (f32[18,18,1]{2,1,0:T(8,128)S(1)}, f32[18,18,1]{2,1,0:T(8,128)S(1)}, u32[]{:S(2)}, u32[]{:S(2)}) collective-permute-start(f32[18,18,1]{2,1,0:T(8,128)S(1)} %get-tuple-element.129), channel_id=1, source_target_pairs={{1,0},{2,1},{3,2},{4,3},{5,4},{6,5},{7,6},{0,7},{9,8},{10,9},{11,1... | collective-permute-start | bytes 3896 | tf_op jit(solution)/shard_map/ppermute | solution.py:22
  83.9 7.1 %collective-permute-start.14 = (f32[3,18,1,128]{3,2,1,0:T(1,128)S(1)}, f32[3,18,1,128]{3,2,1,0:T(1,128)S(1)}, u32[]{:S(2)}, u32[]{:S(2)}) collective-permute-start(f32[3,18,1,128]{3,2,1,0:T(1,128)S(1)} %get-tuple-element.106), channel_id=1, source_target_pairs={{0,8},{8,16},{16,24},{24,32},{32,40},{40,48},{48,56},{56,0},{1,9},... | collective-permute-start | bytes 82952 | tf_op jit(solution)/shard_map/ppermute | solution.py:21
  92.8 7.2 %collective-permute-start.16 = (f32[3,18,18,1]{2,3,1,0:T(1,128)S(1)}, f32[3,18,18,1]{2,3,1,0:T(1,128)S(1)}, u32[]{:S(2)}, u32[]{:S(2)}) collective-permute-start(f32[3,18,18,1]{2,3,1,0:T(1,128)S(1)} %copy.41), channel_id=1, source_target_pairs={{0,1},{1,2},{2,3},{3,4},{4,5},{5,6},{6,7},{7,0},{8,9},{9,10},{10,1... | collective-permute-start | bytes 11672 | tf_op jit(solution)/shard_map/ppermute | solution.py:21
  118.2 7.9 %collective-permute-start.22 = (f32[1,18,18,1]{3,2,1,0:T(8,128)S(1)}, f32[1,18,18,1]{3,2,1,0:T(8,128)S(1)}, u32[]{:S(2)}, u32[]{:S(2)}) collective-permute-start(f32[1,18,18,1]{3,2,1,0:T(8,128)S(1)} %get-tuple-element.126), channel_id=1, source_target_pairs={{0,1},{1,2},{2,3},{3,4},{4,5},{5,6},{6,7},{7,0},{8,9},{9,10},{10,1... | collective-permute-start | bytes 3896 | tf_op jit(solution)/shard_map/ppermute | solution.py:21
  121.5 7.0 %collective-permute-start.23 = (f32[1,18,18,1]{3,2,1,0:T(8,128)S(1)}, f32[1,18,18,1]{3,2,1,0:T(8,128)S(1)}, u32[]{:S(2)}, u32[]{:S(2)}) collective-permute-start(f32[1,18,18,1]{3,2,1,0:T(8,128)S(1)} %get-tuple-element.127), channel_id=1, source_target_pairs={{1,0},{2,1},{3,2},{4,3},{5,4},{6,5},{7,6},{0,7},{9,8},{10,9},{11,1... | collective-permute-start | bytes 3896 | tf_op jit(solution)/shard_map/ppermute | solution.py:22
  143.5 7.9 %collective-permute-start.28 = (f32[1,18,18,1]{3,2,1,0:T(8,128)S(1)}, f32[1,18,18,1]{3,2,1,0:T(8,128)S(1)}, u32[]{:S(2)}, u32[]{:S(2)}) collective-permute-start(f32[1,18,18,1]{3,2,1,0:T(8,128)S(1)} %get-tuple-element.124), channel_id=1, source_target_pairs={{0,1},{1,2},{2,3},{3,4},{4,5},{5,6},{6,7},{7,0},{8,9},{9,10},{10,1... | collective-permute-start | bytes 3896 | tf_op jit(solution)/shard_map/ppermute | solution.py:21
  182.6 7.3 %collective-permute-start.34 = (f32[1,10,10,1]{3,0,2,1:T(1,128)S(1)}, f32[1,10,10,1]{3,0,2,1:T(1,128)S(1)}, u32[]{:S(2)}, u32[]{:S(2)}) collective-permute-start(f32[1,10,10,1]{3,0,2,1:T(1,128)S(1)} %get-tuple-element.160), channel_id=1, source_target_pairs={{0,1},{1,2},{2,3},{3,4},{4,5},{5,6},{6,7},{7,0},{8,9},{9,10},{10,1... | collective-permute-start | bytes 1208 | tf_op jit(solution)/shard_map/ppermute | solution.py:21
  204.8 6.9 %collective-permute-start.40 = (f32[1,10,10,1]{3,0,2,1:T(1,128)S(1)}, f32[1,10,10,1]{3,0,2,1:T(1,128)S(1)}, u32[]{:S(2)}, u32[]{:S(2)}) collective-permute-start(f32[1,10,10,1]{3,0,2,1:T(1,128)S(1)} %get-tuple-element.158), channel_id=1, source_target_pairs={{0,1},{1,2},{2,3},{3,4},{4,5},{5,6},{6,7},{7,0},{8,9},{9,10},{10,1... | collective-permute-start | bytes 1208 | tf_op jit(solution)/shard_map/ppermute | solution.py:21
  228.3 7.0 %collective-permute-start.46 = (f32[1,6,6,1]{3,0,2,1:T(1,128)S(1)}, f32[1,6,6,1]{3,0,2,1:T(1,128)S(1)}, u32[]{:S(2)}, u32[]{:S(2)}) collective-permute-start(f32[1,6,6,1]{3,0,2,1:T(1,128)S(1)} %get-tuple-element.184), channel_id=1, source_target_pairs={{0,1},{1,2},{2,3},{3,4},{4,5},{5,6},{6,7},{7,0},{8,9},{9,10},{10,1... | collective-permute-start | bytes 440 | tf_op jit(solution)/shard_map/ppermute | solution.py:21
  327.2 6.9 %collective-permute-start.72 = (f32[1,1,4,32]{3,2,1,0:T(4,128)S(1)}, f32[1,1,4,32]{3,2,1,0:T(4,128)S(1)}, u32[]{:S(2)}, u32[]{:S(2)}) collective-permute-start(f32[1,1,4,32]{3,2,1,0:T(4,128)S(1)} %get-tuple-element.196), channel_id=1, source_target_pairs={{0,64},{64,128},{128,192},{192,256},{256,320},{320,384},{384,448},... | collective-permute-start | bytes 1544 | tf_op jit(solution)/shard_map/ppermute | solution.py:21
  327.2 7.1 %collective-permute-start.73 = (f32[1,1,4,32]{3,2,1,0:T(4,128)S(1)}, f32[1,1,4,32]{3,2,1,0:T(4,128)S(1)}, u32[]{:S(2)}, u32[]{:S(2)}) collective-permute-start(f32[1,1,4,32]{3,2,1,0:T(4,128)S(1)} %get-tuple-element.197), channel_id=1, source_target_pairs={{64,0},{128,64},{192,128},{256,192},{320,256},{384,320},{448,384},... | collective-permute-start | bytes 1544 | tf_op jit(solution)/shard_map/ppermute | solution.py:22
  349.6 6.9 %collective-permute-start.78 = (f32[1,1,4,32]{3,2,1,0:T(4,128)S(1)}, f32[1,1,4,32]{3,2,1,0:T(4,128)S(1)}, u32[]{:S(2)}, u32[]{:S(2)}) collective-permute-start(f32[1,1,4,32]{3,2,1,0:T(4,128)S(1)} %get-tuple-element.194), channel_id=1, source_target_pairs={{0,64},{64,128},{128,192},{192,256},{256,320},{320,384},{384,448},... | collective-permute-start | bytes 1544 | tf_op jit(solution)/shard_map/ppermute | solution.py:21
  349.6 7.1 %collective-permute-start.79 = (f32[1,1,4,32]{3,2,1,0:T(4,128)S(1)}, f32[1,1,4,32]{3,2,1,0:T(4,128)S(1)}, u32[]{:S(2)}, u32[]{:S(2)}) collective-permute-start(f32[1,1,4,32]{3,2,1,0:T(4,128)S(1)} %get-tuple-element.195), channel_id=1, source_target_pairs={{64,0},{128,64},{192,128},{256,192},{320,256},{384,320},{448,384},... | collective-permute-start | bytes 1544 | tf_op jit(solution)/shard_map/ppermute | solution.py:22
  433.9 8.2 %collective-permute-start.100 = (f32[1,18,18,1]{3,2,1,0:T(8,128)S(1)}, f32[1,18,18,1]{3,2,1,0:T(8,128)S(1)}, u32[]{:S(2)}, u32[]{:S(2)}) collective-permute-start(f32[1,18,18,1]{3,2,1,0:T(8,128)S(1)} %get-tuple-element.122), channel_id=1, source_target_pairs={{0,1},{1,2},{2,3},{3,4},{4,5},{5,6},{6,7},{7,0},{8,9},{9,10},{10,1... | collective-permute-start | bytes 3896 | tf_op jit(solution)/shard_map/ppermute | solution.py:21
  458.7 8.2 %collective-permute-start.106 = (f32[1,18,18,1]{3,2,1,0:T(8,128)S(1)}, f32[1,18,18,1]{3,2,1,0:T(8,128)S(1)}, u32[]{:S(2)}, u32[]{:S(2)}) collective-permute-start(f32[1,18,18,1]{3,2,1,0:T(8,128)S(1)} %get-tuple-element.120), channel_id=1, source_target_pairs={{0,1},{1,2},{2,3},{3,4},{4,5},{5,6},{6,7},{7,0},{8,9},{9,10},{10,1... | collective-permute-start | bytes 3896 | tf_op jit(solution)/shard_map/ppermute | solution.py:21
  461.9 7.0 %collective-permute-start.107 = (f32[1,18,18,1]{3,2,1,0:T(8,128)S(1)}, f32[1,18,18,1]{3,2,1,0:T(8,128)S(1)}, u32[]{:S(2)}, u32[]{:S(2)}) collective-permute-start(f32[1,18,18,1]{3,2,1,0:T(8,128)S(1)} %get-tuple-element.121), channel_id=1, source_target_pairs={{1,0},{2,1},{3,2},{4,3},{5,4},{6,5},{7,6},{0,7},{9,8},{10,9},{11,1... | collective-permute-start | bytes 3896 | tf_op jit(solution)/shard_map/ppermute | solution.py:22
  484.6 8.0 %collective-permute-start.112 = (f32[1,18,18,1]{3,2,1,0:T(8,128)S(1)}, f32[1,18,18,1]{3,2,1,0:T(8,128)S(1)}, u32[]{:S(2)}, u32[]{:S(2)}) collective-permute-start(f32[1,18,18,1]{3,2,1,0:T(8,128)S(1)} %get-tuple-element.118), channel_id=1, source_target_pairs={{0,1},{1,2},{2,3},{3,4},{4,5},{5,6},{6,7},{7,0},{8,9},{9,10},{10,1... | collective-permute-start | bytes 3896 | tf_op jit(solution)/shard_map/ppermute | solution.py:21
  488.2 7.1 %collective-permute-start.113 = (f32[1,18,18,1]{3,2,1,0:T(8,128)S(1)}, f32[1,18,18,1]{3,2,1,0:T(8,128)S(1)}, u32[]{:S(2)}, u32[]{:S(2)}) collective-permute-start(f32[1,18,18,1]{3,2,1,0:T(8,128)S(1)} %get-tuple-element.119), channel_id=1, source_target_pairs={{1,0},{2,1},{3,2},{4,3},{5,4},{6,5},{7,6},{0,7},{9,8},{10,9},{11,1... | collective-permute-start | bytes 3896 | tf_op jit(solution)/shard_map/ppermute | solution.py:22
  (96 other events, 523.5 us)
where the time goes:
time: 503 us; the launch traced here: 497 us
  starting transfers between devices  360 us (72%)
  waiting for transfers between devices  79.1 us (16%)
  local copies, waits for them, and re-layouts  25.4 us (5%)
  other arithmetic  16.8 us (3%)
  matrix products  12.1 us (2%)
    ppermute x57, starting transfers between devices, with_halo(): after = lax.ppermute(initial, axis, down)  207 us
    ppermute x57, starting transfers between devices, with_halo(): before = lax.ppermute(last, axis, up)  154 us
    ppermute x57, waiting for transfers between devices, with_halo(): after = lax.ppermute(initial, axis, down)  59 us
    ppermute x57, waiting for transfers between devices, with_halo(): before = lax.ppermute(last, axis, up)  20.1 us
    reshape x3, local copies, waits for them, and re-layouts, restrict(): fine.reshape(fine.shape[0] // 2, 2, fine.shape[1] // 2, 2, fine.shape[2]...  10.9 us
  transfers between devices with their start and end apart: 114, of which 81 were waited for; matrix products, arithmetic and copies ran while one was open for 1% of the time, Pallas kernels for 0%

commit v1 on v0

v1 whole, which is shorter than its diff:
```python
import jax
import jax.numpy as jnp
from jax import lax
from jax.experimental import pallas as pl
from jax.experimental.pallas import tpu as pltpu
from jax.sharding import PartitionSpec as P

MESH = pl.DeviceIdType.MESH
AXES = ("gx", "gy", "gz")
F32, BF16 = jnp.float32, jnp.bfloat16
EXACT = lax.Precision.HIGHEST

TIME_STEP = 0.1
GAIN = 0.5
C = 0.8 / 6.0

FACES = [(1, 0, 0), (-1, 0, 0), (0, 1, 0), (0, -1, 0), (0, 0, 1), (0, 0, -1)]
AROUND = [
    (i, j, k) for i in (-1, 0, 1) for j in (-1, 0, 1) for k in (-1, 0, 1) if (i, j, k) != (0, 0, 0)
]
PLANE_ROWS = 24
N_COPIES = 6 * 3 + 26 * 2 + 20 + 6


def lanes(shape):
    return lax.broadcasted_iota(jnp.int32, shape, len(shape) - 1)


def rows_of(shape):
    return lax.broadcasted_iota(jnp.int32, shape, len(shape) - 2)


def lane_roll(value, shift):
    return pltpu.roll(value, shift % 128, value.ndim - 1)


def dot(a, b, precision=None):
    return jnp.dot(a, b, precision=precision, preferred_element_type=F32)


def coarse_lane(shape, axis):
    fine = lax.broadcasted_iota(jnp.int32, shape, axis)
    return jnp.where(fine < 192, 32 + fine // 2, fine // 2 - 96)


class Copies:
    def __init__(self, ids, send_sem, recv_sem):
        self.ids, self.send_sem, self.recv_sem = ids, send_sem, recv_sem
        self.made = []

    def device(self, offset):
        return tuple(lax.rem(i + 8 + o, 8) for i, o in zip(self.ids, offset))

    def start(self, src, dst, offset):
        k = len(self.made)
        copy = pltpu.make_async_remote_copy(
            src_ref=src,
            dst_ref=dst,
            send_sem=self.send_sem.at[k],
            recv_sem=self.recv_sem.at[k],
            device_id=self.device(offset),
            device_id_type=MESH,
        )
        copy.start()
        self.made.append(copy)
        return copy


def sum6(ref, base, n, period):
    center = ref[pl.ds(base, n), :]
    total = ref[pl.ds(base + period, n), :] + ref[pl.ds(base - period, n), :]
    total = total + ref[pl.ds(base + 1, n), :] + ref[pl.ds(base - 1, n), :]
    return center, total + lane_roll(center, 1) + lane_roll(center, -1)


def sum6_wide(ref, base, n, period):
    center = [ref[t, pl.ds(base, n), :] for t in (0, 1)]
    lane = lanes((n, 128))
    up = [lane_roll(c, -1) for c in center]
    down = [lane_roll(c, 1) for c in center]
    out = []
    for t in (0, 1):
        total = ref[t, pl.ds(base + period, n), :] + ref[t, pl.ds(base - period, n), :]
        total = total + ref[t, pl.ds(base + 1, n), :] + ref[t, pl.ds(base - 1, n), :]
        total = total + jnp.where(lane == 127, up[1 - t], up[t])
        out.append(total + jnp.where(lane == 0, down[1 - t], down[t]))
    return center, out


def kernel(
    vel, w1, b1, w2, b2, w3, vout, pout,
    w1k, w2k, w3k, b1k, b2k,
    vb, nb, pb, sy, sz, rz,
    dv, sdz, rdx, rdy, rde, rdz, db, v0, u0,
    rs, rt, s1, v1s, r1c, sez, rex, rey, ree, rez, lb1, v1, u1,
    sa, ra, sb, rb, lb2, v2, u2, lb3, v3, u3,
    send_sem, recv_sem,
):
    ids = [lax.axis_index(a) for a in AXES]
    cp = Copies(ids, send_sem, recv_sem)
    barrier = pltpu.get_barrier_semaphore()
    for offset in FACES:
        pl.semaphore_signal(barrier, inc=1, device_id=cp.device(offset), device_id_type=MESH)

    def place(p, carry):
        base = pl.multiple_of(8 + PLANE_ROWS * (p + 1), 8)
        for c in range(3):
            vb[c, pl.ds(base, 16), :] = vel[c, p]
        return carry

    lax.fori_loop(0, 16, place, 0, unroll=True)

    def pack_faces(ref2d, which):
        lane = lanes((16, 128))
        packed = jnp.zeros((16, 128), F32)
        for c, load in enumerate(ref2d):
            sy[which, 0, c] = load(pl.ds(8 + PLANE_ROWS, 16, stride=PLANE_ROWS))
            sy[which, 1, c] = load(pl.ds(8 + PLANE_ROWS + 15, 16, stride=PLANE_ROWS))
            for x in range(16):
                plane = load(pl.ds(8 + PLANE_ROWS * (x + 1), 16))
                packed = jnp.where(lane // 2 == 4 * x + c, lane_roll(plane, 8 * x + 2 * c + 1), packed)
        sz[which] = packed

    pack_faces([lambda d, c=c: vb[c, d, :] for c in range(3)], 0)

    pl.semaphore_wait(barrier, len(FACES))

    low, high = 8, 8 + PLANE_ROWS * 17
    first, last = 8 + PLANE_ROWS, 8 + PLANE_ROWS * 16
    vel_copies = [
        cp.start(vel.at[:, 0], vb.at[:, pl.ds(high, 16), :], (-1, 0, 0)),
        cp.start(vel.at[:, 15], vb.at[:, pl.ds(low, 16), :], (1, 0, 0)),
        cp.start(sy.at[0, 0], rz.at[0, 1], (0, -1, 0)),
        cp.start(sy.at[0, 1], rz.at[0, 0], (0, 1, 0)),
        cp.start(sz.at[0], rz.at[0, 2, 1], (0, 0, -1)),
        cp.start(sz.at[0], rz.at[0, 2, 0], (0, 0, 1)),
    ]

    spread = (rows_of((256, 32)) // 8 == lanes((256, 32))).astype(BF16)
    spread_t = (rows_of((32, 256)) == lanes((32, 256)) // 8).astype(BF16)
    columns = (rows_of((9, 80)) == lanes((9, 80)) // 8).astype(BF16)
    wide = dot(dot(spread, w1[...]).astype(BF16), columns)
    same = rows_of((256, 80)) % 8 == lanes((256, 80)) % 8
    w1k[...] = jnp.where(same, wide, 0.0).astype(BF16)
    wide = dot(dot(spread, w2[...]).astype(BF16), spread_t)
    same = rows_of((256, 256)) % 8 == lanes((256, 256)) % 8
    w2k[...] = jnp.where(same, wide, 0.0).astype(BF16)
    wide = jnp.broadcast_to(dot(w3[...], spread_t), (16, 256))
    same = rows_of((16, 256)) == lanes((16, 256)) % 8
    w3k[...] = jnp.where(same, wide, 0.0).astype(BF16)
    mine = rows_of((256, 32)) // 8 == lanes((256, 32))
    for bias, kept in ((b1, b1k), (b2, b2k)):
        column = jnp.sum(jnp.where(mine, bias[...], 0.0), axis=1, keepdims=True)
        kept[...] = jnp.broadcast_to(column, (256, 128))
    lb2[...] = jnp.zeros_like(lb2)

    for c in vel_copies:
        c.wait_recv()
    for c in range(3):
        vb[c, pl.ds(8 + PLANE_ROWS - 1, 16, stride=PLANE_ROWS), :] = rz[0, 0, c]
        vb[c, pl.ds(8 + PLANE_ROWS + 16, 16, stride=PLANE_ROWS), :] = rz[0, 1, c]

    lane16 = lanes((16, 128))

    def z_next(plane, halo, x, c):
        beyond = pltpu.roll(halo, lax.rem(254 - 8 * x - 2 * c, 128), 1)
        return jnp.where(lane16 == 127, beyond, lane_roll(plane, -1))

    def z_last(plane, halo, x, c):
        beyond = pltpu.roll(halo, lax.rem(256 - 8 * x - 2 * c, 128), 1)
        return jnp.where(lane16 == 0, beyond, lane_roll(plane, 1))

    def neighbours(load, x, base, which, c):
        plane = load(base)
        return plane, [
            (load(base + PLANE_ROWS), load(base - PLANE_ROWS)),
            (load(base + 1), load(base - 1)),
            (z_next(plane, rz[which, 2, 1], x, c), z_last(plane, rz[which, 2, 0], x, c)),
        ]

    def vel_load(c):
        return lambda base: vb[c, pl.ds(base, 16), :]

    def closure(x, carry):
        base = pl.multiple_of(8 + PLANE_ROWS * (x + 1), 8)
        g = []
        for c in range(3):
            _, around = neighbours(vel_load(c), x, base, 0, c)
            g.append([0.5 * (a - b) for a, b in around])
        listing = [
            g[0][0], g[1][1], g[2][2],
            0.5 * (g[0][1] + g[1][0]), 0.5 * (g[0][2] + g[2][0]), 0.5 * (g[1][2] + g[2][1]),
            0.5 * (g[0][1] - g[1][0]), 0.5 * (g[0][2] - g[2][0]), 0.5 * (g[1][2] - g[2][1]),
        ]
        listing.append(jnp.zeros((16, 128), F32))
        features = jnp.concatenate(
            [jnp.concatenate([entry[0:8], entry[8:16]], axis=1) for entry in listing], axis=0
        ).astype(BF16)
        bias = jnp.concatenate([b1k[...]] * 2, axis=1)
        hidden = jnp.tanh(dot(w1k[...], features) + bias).astype(BF16)
        bias = jnp.concatenate([b2k[...]] * 2, axis=1)
        second = jnp.tanh(dot(w2k[...], hidden) + bias).astype(BF16)
        s = dot(w3k[...], second)[0:8]
        soft = GAIN * (jnp.maximum(s, 0.0) + jnp.log1p(jnp.exp(-jnp.abs(s))))
        nb[pl.ds(base, 16), :] = jnp.concatenate([soft[:, 0:128], soft[:, 128:256]], axis=0)
        return carry

    lax.fori_loop(0, 16, closure, 0)

    pack_faces([lambda d: nb[d, :]], 1)
    visc_copies = [
        cp.start(nb.at[pl.ds(first, 16), :], nb.at[pl.ds(high, 16), :], (-1, 0, 0)),
        cp.start(nb.at[pl.ds(last, 16), :], nb.at[pl.ds(low, 16), :], (1, 0, 0)),
        cp.start(sy.at[1, 0, 0], rz.at[1, 1, 0], (0, -1, 0)),
        cp.start(sy.at[1, 1, 0], rz.at[1, 0, 0], (0, 1, 0)),
        cp.start(sz.at[1], rz.at[1, 2, 1], (0, 0, -1)),
        cp.start(sz.at[1], rz.at[1, 2, 0], (0, 0, 1)),
    ]
    for c in visc_copies:
        c.wait_recv()
    nb[pl.ds(8 + PLANE_ROWS - 1, 16, stride=PLANE_ROWS), :] = rz[1, 0, 0]
    nb[pl.ds(8 + PLANE_ROWS + 16, 16, stride=PLANE_ROWS), :] = rz[1, 1, 0]

    def tendency(x, carry):
        base = pl.multiple_of(8 + PLANE_ROWS * (x + 1), 8)
        mid, thick = neighbours(lambda r: nb[pl.ds(r, 16), :], x, base, 1, 0)
        thick = [(0.5 * (mid + a), 0.5 * (mid + b)) for a, b in thick]
        all_v = [neighbours(vel_load(c), x, base, 0, c) for c in range(3)]
        for i in range(3):
            center, around = all_v[i]
            change = 0.0
            for j in range(3):
                (up, down), (up_j, down_j) = around[j], all_v[j][1][j]
                change = change + thick[j][0] * (up - center) - thick[j][1] * (center - down)
                change = change - 0.5 * (up_j * up - down_j * down)
            pb[i, pl.ds(base, 16), :] = center + TIME_STEP * change
        return carry

    lax.fori_loop(0, 16, tendency, 0, unroll=2)

    sy[2, 0, 0] = pb[1, pl.ds(first, 16, stride=PLANE_ROWS), :]
    sy[2, 1, 0] = pb[1, pl.ds(first + 15, 16, stride=PLANE_ROWS), :]
    packed = jnp.zeros((16, 128), F32)
    for x in range(16):
        plane = pb[2, pl.ds(8 + PLANE_ROWS * (x + 1), 16), :]
        packed = jnp.where(lane16 // 2 == 4 * x, lane_roll(plane, 8 * x + 1), packed)
    sz[2] = packed
    prov_copies = [
        cp.start(pb.at[0, pl.ds(first, 16), :], pb.at[0, pl.ds(high, 16), :], (-1, 0, 0)),
        cp.start(pb.at[0, pl.ds(last, 16), :], pb.at[0, pl.ds(low, 16), :], (1, 0, 0)),
        cp.start(sy.at[2, 0, 0], rz.at[2, 1, 0], (0, -1, 0)),
        cp.start(sy.at[2, 1, 0], rz.at[2, 0, 0], (0, 1, 0)),
        cp.start(sz.at[2], rz.at[2, 2, 1], (0, 0, -1)),
        cp.start(sz.at[2], rz.at[2, 2, 0], (0, 0, 1)),
    ]
    for c in prov_copies:
        c.wait_recv()
    pb[1, pl.ds(first - 1, 16, stride=PLANE_ROWS), :] = rz[2, 0, 0]
    pb[1, pl.ds(first + 16, 16, stride=PLANE_ROWS), :] = rz[2, 1, 0]

    for x in range(16):
        base = 8 + PLANE_ROWS * (x + 1)
        plane = pb[2, pl.ds(base, 16), :]
        total = pb[0, pl.ds(base + PLANE_ROWS, 16), :] - pb[0, pl.ds(base - PLANE_ROWS, 16), :]
        total = total + pb[1, pl.ds(base + 1, 16), :] - pb[1, pl.ds(base - 1, 16), :]
        beyond = jnp.where(lane16 == 127, lane_roll(rz[2, 2, 1], 126 - 8 * x), lane_roll(plane, -1))
        before = jnp.where(lane16 == 0, lane_roll(rz[2, 2, 0], -8 * x), lane_roll(plane, 1))
        dv[x] = 0.5 * (total + (beyond - before))

    for half in range(2):
        packed = jnp.zeros((16, 128), F32)
        for k in range(8):
            packed = jnp.where(lane16 // 16 == k, lane_roll(dv[8 * half + k], 16 * k + 8), packed)
        sdz[half] = packed
    div_copies = []
    for dx, dy, dz in AROUND:
        here_x, here_y = (1 - dx) // 2, (1 - dy) // 2
        if dz == 0:
            if dy == 0:
                src, dst = dv.at[pl.ds(10 if dx > 0 else 0, 6)], rdx.at[here_x]
            elif dx == 0:
                src, dst = dv.at[:, pl.ds(8 if dy > 0 else 0, 8), :], rdy.at[here_y]
            else:
                src = dv.at[pl.ds(10 if dx > 0 else 0, 6), pl.ds(8 if dy > 0 else 0, 8), :]
                dst = rde.at[here_x, here_y]
        else:
            half = pl.ds(0, 2) if dx == 0 else pl.ds(1 if dx > 0 else 0, 1)
            slot = pl.ds(1, 2) if dx == 0 else pl.ds(0 if dx > 0 else 3, 1)
            part = pl.ds(0, 16) if dy == 0 else pl.ds(8 if dy > 0 else 0, 8)
            rows = pl.ds(8, 16) if dy == 0 else pl.ds(0 if dy > 0 else 24, 8)
            src, dst = sdz.at[half, part, :], rdz.at[(1 - dz) // 2, slot, rows, :]
        div_copies.append(cp.start(src, dst, (dx, dy, dz)))

    def at0(p):
        return 8 + 32 * p

    for x in range(16):
        db[0, pl.ds(at0(x + 6) + 8, 16), :] = dv[x]
    for c in div_copies:
        c.wait_recv()
    for x in range(6):
        for side, p in ((0, x), (1, 22 + x)):
            db[0, pl.ds(at0(p) + 8, 16), :] = rdx[side, x]
            db[0, pl.ds(at0(p), 8), :] = rde[side, 0, x]
            db[0, pl.ds(at0(p) + 24, 8), :] = rde[side, 1, x]
    for x in range(16):
        db[0, pl.ds(at0(x + 6), 8), :] = rdy[0, x]
        db[0, pl.ds(at0(x + 6) + 24, 8), :] = rdy[1, x]
    lane32 = lanes((32, 128))
    for g in range(4):
        both = jnp.where(lane32 % 16 < 8, rdz[0, g], rdz[1, g])
        for k in range(8):
            x = 8 * (g - 1) + k
            if -6 <= x < 22:
                db[1, pl.ds(at0(x + 6), 32), :] = lane_roll(both, -(16 * k + 8))

    for p in range(1, 27, 2):
        b, around = sum6_wide(db, at0(p), 64, 32)
        for t in (0, 1):
            v0[t, pl.ds(at0(p), 64), :] = -C * (1.2 * b[t] + C * around[t])
    for k in range(12):
        base = at0(2 + 2 * k)
        v, around = sum6_wide(v0, base, 64, 32)
        for t in (0, 1):
            residual = db[t, pl.ds(base, 64), :] - (around[t] - 6.0 * v[t])
            rs[pl.ds(32 * k, 32), pl.ds(128 * t, 128)] = residual[0:32] + residual[32:64]
    halve = jnp.where(coarse_lane((256, 128), 0) == lanes((256, 128)), 0.125, 0.0).astype(F32)
    rt[...] = dot(rs[...], halve, EXACT)
    s1[...] = rt[pl.ds(0, 192, stride=2), :] + rt[pl.ds(1, 192, stride=2), :]

    lane8 = lanes((8, 128))
    packed = jnp.zeros((8, 128), F32)
    for x in range(8):
        plane = s1[pl.ds(16 * (x + 2) + 4, 8), :]
        r1c[x] = plane
        packed = jnp.where(lane8 // 8 == 2 * x, lane_roll(plane, 16 * x - 88), packed)
        packed = jnp.where(lane8 // 8 == 2 * x + 1, lane_roll(plane, 16 * x + 8 - 32), packed)
    sez[...] = packed

    for p in range(1, 11, 5):
        b, around = sum6(s1, 16 * p, 80, 16)
        v1s[pl.ds(16 * p, 80), :] = -4.0 * C * (1.2 * b + C * around)
    parts = []
    for k in range(4):
        base = 16 * (2 + 2 * k)
        v, around = sum6(v1s, base, 32, 16)
        residual = s1[pl.ds(base, 32), :] - 0.25 * (around - 6.0 * v)
        parts.append(residual[0:16] + residual[16:32])
    halve = halve[0:128]
    rt[pl.ds(0, 64), :] = dot(jnp.concatenate(parts, axis=0), halve, EXACT)
    packed = jnp.zeros((8, 128), F32)
    for x in range(4):
        plane = rt[pl.ds(16 * x, 8, stride=2), :] + rt[pl.ds(16 * x + 1, 8, stride=2), :]
        packed = jnp.where(lane8 // 32 == x, lane_roll(plane, 32 * x - 48), packed)
    sa[...] = packed
    ra[3, 1] = packed
    xz_copies = [
        cp.start(sa, ra.at[3 - dx, 1 - dz], (dx, 0, dz))
        for dx in range(-3, 4)
        for dz in (-1, 0, 1)
        if (dx, dz) != (0, 0)
    ]
    src_copies = []
    for dx, dy, dz in AROUND:
        here_x, here_y = (1 - dx) // 2, (1 - dy) // 2
        if dz == 0:
            planes = pl.ds(3 if dx > 0 else 0, 5)
            if dy == 0:
                src, dst = r1c.at[planes], rex.at[here_x]
            elif dx == 0:
                src, dst = r1c, rey.at[here_y]
            else:
                src, dst = r1c.at[planes], ree.at[here_x, here_y]
        else:
            src, dst = sez, rez.at[(1 - dz) // 2, 1 - dx, pl.ds(8 * (1 - dy), 8), :]
        src_copies.append(cp.start(src, dst, (dx, dy, dz)))

    for c in xz_copies:
        c.wait_recv()
    row8 = rows_of((8, 128))
    kept_rows = (row8 >= 2) & (row8 < 6)
    for dx in range(7):
        four = []
        for x in range(4):
            before, here, after = (
                lane_roll(ra[dx, k], lane - 32 * x) for k, lane in ((0, 16), (1, 48), (2, 80))
            )
            whole = jnp.where(lane8 < 48, before, jnp.where(lane8 < 80, here, after))
            lb2[pl.ds(32 * (4 * dx + x) + 12, 4), :] = whole[2:6]
            four.append(whole)
        pairs = [
            jnp.where(lane8 < 64, lane_roll(four[i], -32), lane_roll(four[i + 1], 32)) for i in (0, 2)
        ]
        sb[dx] = jnp.where(kept_rows, pairs[0], pltpu.roll(pairs[1], 4, 0))
    y_copies = []
    for dy in (1, -1, 2, -2, 3, -3):
        wanted = pl.ds(abs(dy) - 1, 9 - 2 * abs(dy))
        y_copies.append(cp.start(sb.at[wanted], rb.at[3 - dy, wanted], (0, dy, 0)))

    for c in src_copies:
        c.wait_recv()
    lane24 = lanes((24, 128))
    for p in range(18):
        dx, x = (p - 5) // 8, (p - 5) % 8
        if dx == 0:
            three = [rey[0, x], r1c[x], rey[1, x]]
        else:
            side = (dx + 1) // 2
            k = x - 3 if dx < 0 else x
            three = [ree[side, 0, k], rex[side, k], ree[side, 1, k]]
        before = lane_roll(rez[0, dx + 1], 24 - 16 * x)
        after = lane_roll(rez[1, dx + 1], 96 - 16 * x - 8)
        here = jnp.concatenate(three, axis=0)
        lb1[pl.ds(24 * p, 24), :] = jnp.where(
            lane24 < 32, before, jnp.where(lane24 < 96, here, after)
        )
    for p in range(1, 17, 4):
        b, around = sum6(lb1, 24 * p, 96, 24)
        v1[pl.ds(24 * p, 96), :] = -4.0 * C * (1.2 * b + C * around)

    for c in y_copies:
        c.wait_recv()
    for dy in (-3, -2, -1, 1, 2, 3):
        for dx in range(abs(dy) - 1, 8 - abs(dy)):
            tile = rb[3 + dy, dx]
            other = pltpu.roll(tile, 4, 0)
            for x in range(4):
                plane = lane_roll(tile if x < 2 else other, 32 if x % 2 == 0 else -32)
                lb2[pl.ds(32 * (4 * dx + x) + 12 + 4 * dy, 4), :] = plane[2:6]

    for p in range(1, 27, 2):
        b, around = sum6(lb2, 32 * p, 64, 32)
        v2[pl.ds(32 * p, 64), :] = -16.0 * C * (1.2 * b + C * around)
    for k in range(12):
        base = 32 * (2 + 2 * k)
        v, around = sum6(v2, base, 64, 32)
        residual = lb2[pl.ds(base, 64), :] - 0.0625 * (around - 6.0 * v)
        rs[pl.ds(32 * k, 32), pl.ds(0, 128)] = residual[0:32] + residual[32:64]
    rt[...] = dot(rs[:, 0:128], halve, EXACT)
    lb3[...] = rt[pl.ds(0, 192, stride=2), :] + rt[pl.ds(1, 192, stride=2), :]

    b, around = sum6(lb3, 16, 160, 16)
    v3[pl.ds(16, 160), :] = -64.0 * C * (1.2 * b + C * around)
    v, around = sum6(v3, 32, 128, 16)
    u3[pl.ds(32, 128), :] = 0.2 * v + C * around - 64.0 * C * lb3[pl.ds(32, 128), :]
    v, around = sum6(u3, 48, 96, 16)
    coarse = 0.2 * v + C * around - 64.0 * C * lb3[pl.ds(48, 96), :]

    double = jnp.where(rows_of((128, 256)) == coarse_lane((128, 256), 1), 1.0, 0.0).astype(F32)
    fine = dot(coarse, double[:, 0:128], EXACT)
    for k in range(6):
        for p in (8 + 2 * k, 9 + 2 * k):
            for odd in (0, 1):
                where = pl.ds(32 * p + odd, 16, stride=2)
                v2[where, :] = v2[where, :] + fine[16 * k : 16 * k + 16]
    for p in range(9, 19, 2):
        v, around = sum6(v2, 32 * p, 64, 32)
        u2[pl.ds(32 * p, 64), :] = 0.2 * v + C * around - 16.0 * C * lb2[pl.ds(32 * p, 64), :]
    for k in range(4):
        base = 32 * (10 + 2 * k)
        v, around = sum6(u2, base, 64, 32)
        rs[pl.ds(64 * k, 64), pl.ds(0, 128)] = (
            0.2 * v + C * around - 16.0 * C * lb2[pl.ds(base, 64), :]
        )

    fine = dot(rs[0:256, 0:128], double[:, 0:128], EXACT)
    for k in range(8):
        for p in (1 + 2 * k, 2 + 2 * k):
            for odd in (0, 1):
                where = pl.ds(24 * p + odd, 12, stride=2)
                v1[where, :] = v1[where, :] + fine[32 * k + 8 : 32 * k + 20]
    for p in range(2, 16, 2):
        v, around = sum6(v1, 24 * p, 48, 24)
        u1[pl.ds(24 * p, 48), :] = 0.2 * v + C * around - 4.0 * C * lb1[pl.ds(24 * p, 48), :]
    for k in range(6):
        base = 24 * (3 + 2 * k)
        v, around = sum6(u1, base, 48, 24)
        rs[pl.ds(48 * k, 48), pl.ds(0, 128)] = (
            0.2 * v + C * around - 4.0 * C * lb1[pl.ds(base, 48), :]
        )

    for t in (0, 1):
        fine = dot(rs[0:288, 0:128], double[:, 128 * t : 128 * t + 128], EXACT)
        for k in range(12):
            for p in (2 + 2 * k, 3 + 2 * k):
                for odd in (0, 1):
                    where = pl.ds(at0(p) + odd, 16, stride=2)
                    v0[t, where, :] = v0[t, where, :] + fine[24 * k + 4 : 24 * k + 20]
    for p in range(4, 24, 2):
        v, around = sum6_wide(v0, at0(p), 64, 32)
        for t in (0, 1):
            b = db[t, pl.ds(at0(p), 64), :]
            u0[t, pl.ds(at0(p), 64), :] = 0.2 * v[t] + C * around[t] - C * b
    for p in range(5, 23, 2):
        v, around = sum6_wide(u0, at0(p), 64, 32)
        for t in (0, 1):
            b = db[t, pl.ds(at0(p), 64), :]
            v0[t, pl.ds(at0(p), 64), :] = 0.2 * v[t] + C * around[t] - C * b

    for x in range(16):
        base = at0(x + 6) + 8
        here, beyond = v0[0, pl.ds(base, 16), :], v0[1, pl.ds(base, 16), :]
        pout[x] = here
        slopes = [
            v0[0, pl.ds(base + 32, 16), :] - v0[0, pl.ds(base - 32, 16), :],
            v0[0, pl.ds(base + 1, 16), :] - v0[0, pl.ds(base - 1, 16), :],
            jnp.where(lane16 == 127, lane_roll(beyond, -1), lane_roll(here, -1))
            - jnp.where(lane16 == 0, lane_roll(beyond, 1), lane_roll(here, 1)),
        ]
        for c in range(3):
            vout[c, x] = pb[c, pl.ds(8 + PLANE_ROWS * (x + 1), 16), :] - 0.5 * slopes[c]

    for c in cp.made:
        c.wait_send()


def body(velocity, input_weight, input_bias, hidden_weight, hidden_bias, output_weight):
    def scratch(*shape):
        return pltpu.VMEM(shape, F32)

    plane_buffer = 16 + PLANE_ROWS * 18
    level0 = 16 + 32 * 28
    return pl.pallas_call(
        kernel,
        out_shape=(
            jax.ShapeDtypeStruct((3, 16, 16, 128), F32),
            jax.ShapeDtypeStruct((16, 16, 128), F32),
        ),
        in_specs=[pl.BlockSpec(memory_space=pltpu.VMEM)] * 6,
        out_specs=[pl.BlockSpec(memory_space=pltpu.VMEM)] * 2,
        scratch_shapes=[
            pltpu.VMEM((256, 80), BF16),
            pltpu.VMEM((256, 256), BF16),
            pltpu.VMEM((16, 256), BF16),
            scratch(256, 128),
            scratch(256, 128),
            scratch(3, plane_buffer, 128),
            scratch(plane_buffer, 128),
            scratch(3, plane_buffer, 128),
            scratch(3, 2, 3, 16, 128),
            scratch(3, 16, 128),
            scratch(3, 3, 3, 16, 128),
            scratch(16, 16, 128),
            scratch(2, 16, 128),
            scratch(2, 6, 16, 128),
            scratch(2, 16, 8, 128),
            scratch(2, 2, 6, 8, 128),
            scratch(2, 4, 32, 128),
            scratch(2, level0, 128),
            scratch(2, level0, 128),
            scratch(2, level0, 128),
            scratch(384, 256),
            scratch(384, 128),
            scratch(192, 128),
            scratch(192, 128),
            scratch(8, 8, 128),
            scratch(8, 128),
            scratch(2, 5, 8, 128),
            scratch(2, 8, 8, 128),
            scratch(2, 2, 5, 8, 128),
            scratch(2, 3, 24, 128),
            scratch(432, 128),
            scratch(432, 128),
            scratch(432, 128),
            scratch(8, 128),
            scratch(7, 3, 8, 128),
            scratch(7, 8, 128),
            scratch(7, 7, 8, 128),
            scratch(896, 128),
            scratch(896, 128),
            scratch(896, 128),
            scratch(192, 128),
            scratch(192, 128),
            scratch(192, 128),
            pltpu.SemaphoreType.DMA((N_COPIES,)),
            pltpu.SemaphoreType.DMA((N_COPIES,)),
        ],
        compiler_params=pltpu.CompilerParams(
            collective_id=0, has_side_effects=True, vmem_limit_bytes=48 * 1024 * 1024
        ),
    )(
        velocity,
        input_weight,
        input_bias.reshape(1, 32),
        hidden_weight,
        hidden_bias.reshape(1, 32),
        output_weight.reshape(1, 32),
    )


def solution(mesh):
    return jax.shard_map(
        body,
        mesh=mesh,
        in_specs=(P(None, "gx", "gy", "gz"), P(), P(), P(), P(), P()),
        out_specs=(P(None, "gx", "gy", "gz"), P("gx", "gy", "gz")),
        check_vma=False,
    )
```

time: 503 us -> 60.8 us (0.12); the launches traced: 497 us -> 60.5 us
  starting transfers between devices: 360 us -> 0 us
  waiting for transfers between devices: 79.1 us -> 0 us
  Pallas kernels: 0 us -> 56.1 us
  local copies, waits for them, and re-layouts: 25.4 us -> 3.75 us
  other arithmetic: 16.8 us -> 0 us
  matrix products: 12.1 us -> 0 us
    ppermute x114 -> x0, starting transfers between devices: 360 us -> none  [the longest x57 207 us: with_halo(): after = lax.ppermute(initial, axis, down)]
    ppermute x114 -> x0, waiting for transfers between devices: 79.1 us -> none  [the longest x57 59 us: with_halo(): after = lax.ppermute(initial, axis, down)]
    pallas_call x0 -> x1, Pallas kernels: none -> 56.1 us  [body(): pl.pallas_call(kernel, out_shape=(jax.ShapeDtypeStruct((3, 16, 16, 128),...]
    dot_general x16 -> x0, matrix products: 12.1 us -> none  [the longest x8 9.46 us: apply_block(): jnp.dot(input_weight, block_cells, preferred_element_type=jnp.float32)]
    reshape x10 -> x0, local copies, waits for them, and re-layouts: 12.1 us -> none  [the longest x3 10.9 us: restrict(): fine.reshape(fine.shape[0] // 2, 2, fine.shape[1] // 2, 2, fine.shape[2]...]
    slice x54 -> x0, local copies, waits for them, and re-layouts: 5.18 us -> none  [the longest x51 3.57 us: with_halo(): last = lax.slice_in_dim(array, length - width, length, axis=dim)]
  transfers between devices with their start and end apart: 114 -> 0, of which waited for: 81 -> 0; matrix products, arithmetic and copies ran while one was open for 1% -> 0% of each run, Pallas kernels for 0% -> 0%
where the time goes in v1:
time: 60.8 us; the launch traced here: 60.5 us
  Pallas kernels  56.1 us (92%)
  local copies, waits for them, and re-layouts  3.75 us (6%)
  between operations  0.66 us (1%)
    pallas_call x1, Pallas kernels, body(): pl.pallas_call(kernel, out_shape=(jax.ShapeDtypeStruct((3, 16, 16, 128),...  56.1 us
    unnamed x15, local copies, waits for them, and re-layouts  3.75 us

profile of v1, /device:TPU:1, one launch (start us, length us, event | category | flops | bytes accessed | tf_op | source)
XLA Modules:
  0.0 60.5 jit_solution(16344370346639098176)
XLA Ops:
  0.6 0.0 copy-start.5
  0.6 0.0 copy-start.1
  0.7 0.7 %copy-done.5 = bf16[32,9]{0,1:T(8,128)(2,1)S(1)} copy-done((bf16[32,9]{0,1:T(8,128)(2,1)S(1)}, bf16[32,9]{0,1:T(8,128)(2,1)}, u32[]{:S(2)}) %copy-start.5) | copy-done | bytes 600
  1.3 0.0 copy-start.2
  1.3 0.0 copy-start.3
  1.3 0.0 copy-start.4
  1.3 0.1 copy.8.w1
  1.4 0.0 copy-done.1
  1.4 0.5 copy-done.2
  2.0 0.0 copy-done.3
  2.0 0.0 copy-done.4
  2.0 0.0 copy-start
  2.0 1.0 %copy-done = f32[3,16,16,128]{3,2,1,0:T(8,128)S(1)} copy-done((f32[3,16,16,128]{3,2,1,0:T(8,128)S(1)}, f32[3,16,16,128]{3,2,1,0:T(8,128)}, u32[]{:S(2)}) %copy-start) | copy-done | bytes 393240
  3.0 56.1 %shard_map.77 = (f32[3,16,16,128]{3,2,1,0:T(8,128)S(1)}, f32[16,16,128]{2,1,0:T(8,128)S(1)}) custom-call(f32[3,16,16,128]{3,2,1,0:T(8,128)S(1)} %copy-done, bf16[32,9]{1,0:T(8,128)(2,1)S(1)} %copy.8.w1, f32[1,32]{1,0:T(1,128)S(1)} %bitcast.3, bf16[32,32]{1,0:T(8,128)(2,1)S(1)} %copy-done.1, f32[1,32]{1,0:T(1,128)S(1)} %bitcast.4, bf16[1,32]{1,0:T(2,128)(2,1)S(1)} %bitcast.5), custom_call_target="tpu_custom_call" | custom-call | tf_op jit(solution)/shard_map/pallas_call | solution.py:523
  59.1 0.7 %copy.11 = f32[3,16,16,128]{3,2,1,0:T(8,128)} copy(f32[3,16,16,128]{3,2,1,0:T(8,128)S(1)} %get-tuple-element.4) | data formatting | bytes 786432
  59.9 0.7 %copy.12 = f32[16,16,128]{2,1,0:T(8,128)} copy(f32[16,16,128]{2,1,0:T(8,128)S(1)} %get-tuple-element.5) | data formatting | bytes 262144
Async XLA Ops:
  0.6 0.7 %copy-start.5 = (bf16[32,9]{0,1:T(8,128)(2,1)S(1)}, bf16[32,9]{0,1:T(8,128)(2,1)}, u32[]{:S(2)}) copy-start(bf16[32,9]{0,1:T(8,128)(2,1)} %param.7) | copy-start | bytes 1732
  0.6 0.8 %copy-start.1 = (bf16[32,32]{1,0:T(8,128)(2,1)S(1)}, bf16[32,32]{1,0:T(8,128)(2,1)}, u32[]{:S(2)}) copy-start(bf16[32,32]{1,0:T(8,128)(2,1)} %w2.1) | copy-start | bytes 6148
  1.3 0.7 %copy-start.2 = (f32[32]{0:T(128)S(1)}, f32[32]{0:T(128)}, u32[]{:S(2)}) copy-start(f32[32]{0:T(128)} %param.8) | copy-start | bytes 388
  1.3 0.7 %copy-start.3 = (f32[32]{0:T(128)S(1)}, f32[32]{0:T(128)}, u32[]{:S(2)}) copy-start(f32[32]{0:T(128)} %param.10) | copy-start | bytes 388
  1.3 0.7 %copy-start.4 = (bf16[32]{0:T(256)(128)(2,1)S(1)}, bf16[32]{0:T(256)(128)(2,1)}, u32[]{:S(2)}) copy-start(bf16[32]{0:T(256)(128)(2,1)} %param.11) | copy-start | bytes 196
  2.0 1.0 %copy-start = (f32[3,16,16,128]{3,2,1,0:T(8,128)S(1)}, f32[3,16,16,128]{3,2,1,0:T(8,128)}, u32[]{:S(2)}) copy-start(f32[3,16,16,128]{3,2,1,0:T(8,128)} %vel.1) | copy-start | bytes 1179652

commit v2 on v1

--- a/solution.py
+++ b/solution.py
@@ -88,13 +88,13 @@
 
 
 def kernel(
-    vel, w1, b1, w2, b2, w3, vout, pout,
-    w1k, w2k, w3k, b1k, b2k,
+    vel_in, w1_in, b1_in, w2_in, b2_in, w3_in, vout, pout,
+    vel, w1, b1, w2, b2, w3, w1k, w2k, w3k, b1k, b2k,
     vb, nb, pb, sy, sz, rz,
     dv, sdz, rdx, rdy, rde, rdz, db, v0, u0,
     rs, rt, s1, v1s, r1c, sez, rex, rey, ree, rez, lb1, v1, u1,
     sa, ra, sb, rb, lb2, v2, u2, lb3, v3, u3,
-    send_sem, recv_sem,
+    send_sem, recv_sem, load_sem,
 ):
     ids = [lax.axis_index(a) for a in AXES]
     cp = Copies(ids, send_sem, recv_sem)
@@ -102,13 +102,18 @@
     for offset in FACES:
         pl.semaphore_signal(barrier, inc=1, device_id=cp.device(offset), device_id_type=MESH)
 
-    def place(p, carry):
-        base = pl.multiple_of(8 + PLANE_ROWS * (p + 1), 8)
-        for c in range(3):
-            vb[c, pl.ds(base, 16), :] = vel[c, p]
-        return carry
-
-    lax.fori_loop(0, 16, place, 0, unroll=True)
+    loads = [
+        pltpu.make_async_copy(src, dst, load_sem.at[k])
+        for k, (src, dst) in enumerate(
+            ((vel_in, vel), (w1_in, w1), (b1_in, b1), (w2_in, w2), (b2_in, b2), (w3_in, w3))
+        )
+    ]
+    for load in loads:
+        load.start()
+    loads[0].wait()
+    for c in range(3):
+        for x in range(16):
+            vb[c, pl.ds(8 + PLANE_ROWS * (x + 1), 16), :] = vel[c, x]
 
     def pack_faces(ref2d, which):
         lane = lanes((16, 128))
@@ -136,10 +141,14 @@
         cp.start(sz.at[0], rz.at[0, 2, 0], (0, 0, 1)),
     ]
 
+    for load in loads[1:]:
+        load.wait()
     spread = (rows_of((256, 32)) // 8 == lanes((256, 32))).astype(BF16)
     spread_t = (rows_of((32, 256)) == lanes((32, 256)) // 8).astype(BF16)
-    columns = (rows_of((9, 80)) == lanes((9, 80)) // 8).astype(BF16)
-    wide = dot(dot(spread, w1[...]).astype(BF16), columns)
+    columns = (rows_of((80, 9)) // 8 == lanes((80, 9))).astype(BF16)
+    wide = lax.dot_general(
+        spread, dot(columns, w1[...]).astype(BF16), (((1,), (1,)), ((), ())), preferred_element_type=F32
+    )
     same = rows_of((256, 80)) % 8 == lanes((256, 80)) % 8
     w1k[...] = jnp.where(same, wide, 0.0).astype(BF16)
     wide = dot(dot(spread, w2[...]).astype(BF16), spread_t)
@@ -163,11 +172,11 @@
     lane16 = lanes((16, 128))
 
     def z_next(plane, halo, x, c):
-        beyond = pltpu.roll(halo, lax.rem(254 - 8 * x - 2 * c, 128), 1)
+        beyond = pltpu.roll(halo, (254 - 8 * x - 2 * c) % 128, 1)
         return jnp.where(lane16 == 127, beyond, lane_roll(plane, -1))
 
     def z_last(plane, halo, x, c):
-        beyond = pltpu.roll(halo, lax.rem(256 - 8 * x - 2 * c, 128), 1)
+        beyond = pltpu.roll(halo, (256 - 8 * x - 2 * c) % 128, 1)
         return jnp.where(lane16 == 0, beyond, lane_roll(plane, 1))
 
     def neighbours(load, x, base, which, c):
@@ -181,31 +190,34 @@
     def vel_load(c):
         return lambda base: vb[c, pl.ds(base, 16), :]
 
-    def closure(x, carry):
-        base = pl.multiple_of(8 + PLANE_ROWS * (x + 1), 8)
-        g = []
-        for c in range(3):
-            _, around = neighbours(vel_load(c), x, base, 0, c)
-            g.append([0.5 * (a - b) for a, b in around])
-        listing = [
-            g[0][0], g[1][1], g[2][2],
-            0.5 * (g[0][1] + g[1][0]), 0.5 * (g[0][2] + g[2][0]), 0.5 * (g[1][2] + g[2][1]),
-            0.5 * (g[0][1] - g[1][0]), 0.5 * (g[0][2] - g[2][0]), 0.5 * (g[1][2] - g[2][1]),
-        ]
-        listing.append(jnp.zeros((16, 128), F32))
+    for first_x in range(0, 16, 4):
+        listing = [[] for _ in range(10)]
+        for x in range(first_x, first_x + 4):
+            base = 8 + PLANE_ROWS * (x + 1)
+            g = []
+            for c in range(3):
+                _, around = neighbours(vel_load(c), x, base, 0, c)
+                g.append([0.5 * (a - b) for a, b in around])
+            entries = [
+                g[0][0], g[1][1], g[2][2],
+                0.5 * (g[0][1] + g[1][0]), 0.5 * (g[0][2] + g[2][0]), 0.5 * (g[1][2] + g[2][1]),
+                0.5 * (g[0][1] - g[1][0]), 0.5 * (g[0][2] - g[2][0]), 0.5 * (g[1][2] - g[2][1]),
+                jnp.zeros((16, 128), F32),
+            ]
+            for tiles, entry in zip(listing, entries):
+                tiles += [entry[0:8], entry[8:16]]
         features = jnp.concatenate(
-            [jnp.concatenate([entry[0:8], entry[8:16]], axis=1) for entry in listing], axis=0
+            [jnp.concatenate(tiles, axis=1) for tiles in listing], axis=0
         ).astype(BF16)
-        bias = jnp.concatenate([b1k[...]] * 2, axis=1)
+        bias = jnp.concatenate([b1k[...]] * 8, axis=1)
         hidden = jnp.tanh(dot(w1k[...], features) + bias).astype(BF16)
-        bias = jnp.concatenate([b2k[...]] * 2, axis=1)
+        bias = jnp.concatenate([b2k[...]] * 8, axis=1)
         second = jnp.tanh(dot(w2k[...], hidden) + bias).astype(BF16)
         s = dot(w3k[...], second)[0:8]
         soft = GAIN * (jnp.maximum(s, 0.0) + jnp.log1p(jnp.exp(-jnp.abs(s))))
-        nb[pl.ds(base, 16), :] = jnp.concatenate([soft[:, 0:128], soft[:, 128:256]], axis=0)
-        return carry
-
-    lax.fori_loop(0, 16, closure, 0)
+        for k in range(8):
+            row = 8 + PLANE_ROWS * (first_x + k // 2 + 1) + 8 * (k % 2)
+            nb[pl.ds(row, 8), :] = soft[:, 128 * k : 128 * k + 128]
 
     pack_faces([lambda d: nb[d, :]], 1)
     visc_copies = [
@@ -221,8 +233,8 @@
     nb[pl.ds(8 + PLANE_ROWS - 1, 16, stride=PLANE_ROWS), :] = rz[1, 0, 0]
     nb[pl.ds(8 + PLANE_ROWS + 16, 16, stride=PLANE_ROWS), :] = rz[1, 1, 0]
 
-    def tendency(x, carry):
-        base = pl.multiple_of(8 + PLANE_ROWS * (x + 1), 8)
+    for x in range(16):
+        base = 8 + PLANE_ROWS * (x + 1)
         mid, thick = neighbours(lambda r: nb[pl.ds(r, 16), :], x, base, 1, 0)
         thick = [(0.5 * (mid + a), 0.5 * (mid + b)) for a, b in thick]
         all_v = [neighbours(vel_load(c), x, base, 0, c) for c in range(3)]
@@ -234,9 +246,6 @@
                 change = change + thick[j][0] * (up - center) - thick[j][1] * (center - down)
                 change = change - 0.5 * (up_j * up - down_j * down)
             pb[i, pl.ds(base, 16), :] = center + TIME_STEP * change
-        return carry
-
-    lax.fori_loop(0, 16, tendency, 0, unroll=2)
 
     sy[2, 0, 0] = pb[1, pl.ds(first, 16, stride=PLANE_ROWS), :]
     sy[2, 1, 0] = pb[1, pl.ds(first + 15, 16, stride=PLANE_ROWS), :]
@@ -523,12 +532,18 @@
     return pl.pallas_call(
         kernel,
         out_shape=(
-            jax.ShapeDtypeStruct((3, 16, 16, 128), F32),
-            jax.ShapeDtypeStruct((16, 16, 128), F32),
+            pltpu.VMEM((3, 16, 16, 128), F32),
+            pltpu.VMEM((16, 16, 128), F32),
         ),
-        in_specs=[pl.BlockSpec(memory_space=pltpu.VMEM)] * 6,
+        in_specs=[pl.BlockSpec(memory_space=pltpu.HBM)] * 6,
         out_specs=[pl.BlockSpec(memory_space=pltpu.VMEM)] * 2,
         scratch_shapes=[
+            scratch(3, 16, 16, 128),
+            pltpu.VMEM((9, 32), BF16),
+            scratch(1, 32),
+            pltpu.VMEM((32, 32), BF16),
+            scratch(1, 32),
+            pltpu.VMEM((1, 32), BF16),
             pltpu.VMEM((256, 80), BF16),
             pltpu.VMEM((256, 256), BF16),
             pltpu.VMEM((16, 256), BF16),
@@ -574,13 +589,14 @@
             scratch(192, 128),
             pltpu.SemaphoreType.DMA((N_COPIES,)),
             pltpu.SemaphoreType.DMA((N_COPIES,)),
+            pltpu.SemaphoreType.DMA((6,)),
         ],
         compiler_params=pltpu.CompilerParams(
-            collective_id=0, has_side_effects=True, vmem_limit_bytes=48 * 1024 * 1024
+            collective_id=0, has_side_effects=True, vmem_limit_bytes=60 * 1024 * 1024
         ),
     )(
         velocity,
-        input_weight,
+        input_weight.T,
         input_bias.reshape(1, 32),
         hidden_weight,
         hidden_bias.reshape(1, 32),

time: 60.8 us -> 49.9 us (0.82)
  Pallas kernels: 56.1 us -> 47.7 us
  local copies, waits for them, and re-layouts: 3.75 us -> 1.4 us
    pallas_call x1, Pallas kernels: 56.1 us -> 47.7 us  [body(): pl.pallas_call(kernel, out_shape=(pltpu.VMEM((3, 16, 16, 128), F32), pltp...]
    unnamed x15 -> x2, local copies, waits for them, and re-layouts: 3.75 us -> 1.4 us
where the time goes in v2:
time: 49.9 us; the launch traced here: 49.7 us
  Pallas kernels  47.7 us (96%)
  local copies, waits for them, and re-layouts  1.4 us (3%)
  between operations  0.64 us (1%)
    pallas_call x1, Pallas kernels, body(): pl.pallas_call(kernel, out_shape=(pltpu.VMEM((3, 16, 16, 128), F32), pltp...  47.7 us
    unnamed x2, local copies, waits for them, and re-layouts  1.4 us

profile of v2, /device:TPU:1, one launch (start us, length us, event | category | flops | bytes accessed | tf_op | source)
XLA Modules:
  0.0 49.7 jit_solution(7057468240064732984)
XLA Ops:
  0.6 47.7 %shard_map.77 = (f32[3,16,16,128]{3,2,1,0:T(8,128)S(1)}, f32[16,16,128]{2,1,0:T(8,128)S(1)}) custom-call(f32[3,16,16,128]{3,2,1,0:T(8,128)} %vel_in.1, bf16[9,32]{1,0:T(8,128)(2,1)} %bitcast.4, f32[1,32]{1,0:T(1,128)} %bitcast.5, bf16[32,32]{1,0:T(8,128)(2,1)} %w2_in.1, f32[1,32]{1,0:T(1,128)} %bitcast.6, bf16[1,32]{1,0:T(2,128)(2,1)} %bitcast.7), custom_call_target="tpu_custom_call" | custom-call | tf_op jit(solution)/shard_map/pallas_call | solution.py:532
  48.3 0.7 %copy.10 = f32[3,16,16,128]{3,2,1,0:T(8,128)} copy(f32[3,16,16,128]{3,2,1,0:T(8,128)S(1)} %get-tuple-element.2) | data formatting | bytes 786432
  49.1 0.7 %copy.11 = f32[16,16,128]{2,1,0:T(8,128)} copy(f32[16,16,128]{2,1,0:T(8,128)S(1)} %get-tuple-element.3) | data formatting | bytes 262144

commit v3 on v2

v3 whole, which is shorter than its diff:
```python
import jax
import jax.numpy as jnp
from jax import lax
from jax.experimental import pallas as pl
from jax.experimental.pallas import tpu as pltpu
from jax.sharding import PartitionSpec as P

MESH = pl.DeviceIdType.MESH
AXES = ("gx", "gy", "gz")
F32, BF16 = jnp.float32, jnp.bfloat16

TIME_STEP = 0.1
GAIN = 0.5
C = 0.8 / 6.0

FACES = [(1, 0, 0), (-1, 0, 0), (0, 1, 0), (0, -1, 0), (0, 0, 1), (0, 0, -1)]
AROUND = [
    (i, j, k) for i in (-1, 0, 1) for j in (-1, 0, 1) for k in (-1, 0, 1) if (i, j, k) != (0, 0, 0)
]
PLANE_ROWS = 24
NEAR = [(a, b) for a in range(5) for b in range(5) if a + b <= 4]
CORNER = [(i, j, k, o) for i in (0, 1) for j in (0, 1) for k, o in enumerate(NEAR)]
EDGES = [o for o in AROUND if abs(o[0]) + abs(o[1]) + abs(o[2]) == 2]
N_COPIES = 6 + 16 + 20 + 26 * 2 + 20 + 6


def at(x, y=0):
    return 8 + PLANE_ROWS * (x + 2) + y


def column(y):
    return pl.ds(at(0, y), 16, stride=PLANE_ROWS)


def at0(p):
    return 8 + 32 * p


def lanes(shape):
    return lax.broadcasted_iota(jnp.int32, shape, len(shape) - 1)


def rows_of(shape):
    return lax.broadcasted_iota(jnp.int32, shape, len(shape) - 2)


def lane_roll(value, shift):
    return pltpu.roll(value, shift % 128, value.ndim - 1)


def dot(a, b, precision=None):
    return jnp.dot(a, b, precision=precision, preferred_element_type=F32)


def coarse_lane(shape, axis):
    fine = lax.broadcasted_iota(jnp.int32, shape, axis)
    return jnp.where(fine < 192, 32 + fine // 2, fine // 2 - 96)


def exact_dot(a, b):
    b = b.astype(BF16)
    first = a.astype(BF16)
    rest = a - first.astype(F32)
    second = rest.astype(BF16)
    third = (rest - second.astype(F32)).astype(BF16)
    return dot(third, b) + dot(second, b) + dot(first, b)


class Copies:
    def __init__(self, ids, send_sem, recv_sem):
        self.ids, self.send_sem, self.recv_sem = ids, send_sem, recv_sem
        self.made, self.count = [], 0

    def device(self, offset):
        return tuple(lax.rem(i + 8 + o, 8) for i, o in zip(self.ids, offset))

    def start(self, src, dst, offset):
        k = self.count + len(self.made)
        copy = pltpu.make_async_remote_copy(
            src_ref=src,
            dst_ref=dst,
            send_sem=self.send_sem.at[k],
            recv_sem=self.recv_sem.at[k],
            device_id=self.device(offset),
            device_id_type=MESH,
        )
        copy.start()
        self.made.append(copy)
        return copy

    def sent(self):
        for copy in self.made:
            copy.wait_send()
        self.count += len(self.made)
        self.made = []


def sum6(ref, base, n, period):
    center = ref[pl.ds(base, n), :]
    total = ref[pl.ds(base + period, n), :] + ref[pl.ds(base - period, n), :]
    total = total + ref[pl.ds(base + 1, n), :] + ref[pl.ds(base - 1, n), :]
    return center, total + lane_roll(center, 1) + lane_roll(center, -1)


def sum6_wide(ref, base, n, period):
    center = [ref[t, pl.ds(base, n), :] for t in (0, 1)]
    lane = lanes((n, 128))
    up = [lane_roll(c, -1) for c in center]
    down = [lane_roll(c, 1) for c in center]
    out = []
    for t in (0, 1):
        total = ref[t, pl.ds(base + period, n), :] + ref[t, pl.ds(base - period, n), :]
        total = total + ref[t, pl.ds(base + 1, n), :] + ref[t, pl.ds(base - 1, n), :]
        total = total + jnp.where(lane == 127, up[1 - t], up[t])
        out.append(total + jnp.where(lane == 0, down[1 - t], down[t]))
    return center, out


def kernel(
    vel_in, w1_in, b1_in, w2_in, b2_in, w3_in, vout, pout,
    vel, w1, b1, w2, b2, w3, w1k, w2k, w3k, b1k, b2k,
    vb, nb, pb, sy, sz, sxy, ry, rz, rxy, rxz, syn, szn, sxyn, ryn, rxyn, cz, zb,
    dv, dvr, sdy, sde, sdz, rdx, rdy, rde, rdz, db, v0, u0,
    rs, rt, s1, v1s, r1c, sez, rex, rey, ree, rez, lb1, v1, u1,
    sa, ra, sb, rb, lb2, v2, u2, lb3, v3, u3,
    send_sem, recv_sem, load_sem,
):
    ids = [lax.axis_index(a) for a in AXES]
    cp = Copies(ids, send_sem, recv_sem)
    barrier = pltpu.get_barrier_semaphore()
    for offset in FACES:
        pl.semaphore_signal(barrier, inc=1, device_id=cp.device(offset), device_id_type=MESH)

    loads = [
        pltpu.make_async_copy(src, dst, load_sem.at[k])
        for k, (src, dst) in enumerate(
            ((vel_in, vel), (w1_in, w1), (b1_in, b1), (w2_in, w2), (b2_in, b2), (w3_in, w3))
        )
    ]
    for load in loads:
        load.start()
    loads[0].wait()
    for c in range(3):
        for x in range(16):
            vb[c, pl.ds(at(x), 16), :] = vel[c, x]

    lane16 = lanes((16, 128))

    def pack_z(plane_of):
        packed = jnp.zeros((16, 128), F32)
        for x in range(16):
            plane = plane_of(x)
            packed = jnp.where(lane16 // 2 == 4 * x + 1, lane_roll(plane, 8 * x + 2), packed)
            packed = jnp.where(lane16 // 2 == 4 * x + 2, lane_roll(plane, 8 * x + 6), packed)
        return packed

    for c in range(3):
        for k, y in enumerate((0, 1, 14, 15)):
            sy[k, c] = vb[c, column(y), :]
        sz[c] = pack_z(lambda x: vel[c, x])
        for i in (0, 1):
            for j in (0, 1):
                sxy[i, j, pl.ds(c, 1), :] = vel[c, 15 * i, pl.ds(15 * j, 1), :]

    pl.semaphore_wait(barrier, len(FACES))

    vel_copies = [
        cp.start(sz, rz.at[0, pl.ds(0, 3), pl.ds(8, 16), :], (0, 0, 1)),
        cp.start(sz, rz.at[1, pl.ds(0, 3), pl.ds(8, 16), :], (0, 0, -1)),
        cp.start(sy.at[3], ry.at[1], (0, 1, 0)),
        cp.start(sy.at[0], ry.at[2], (0, -1, 0)),
        cp.start(vel.at[:, 15], vb.at[:, pl.ds(at(-1), 16), :], (1, 0, 0)),
        cp.start(vel.at[:, 0], vb.at[:, pl.ds(at(16), 16), :], (-1, 0, 0)),
    ]

    for load in loads[1:]:
        load.wait()
    spread = (rows_of((256, 32)) // 8 == lanes((256, 32))).astype(BF16)
    spread_t = (rows_of((32, 256)) == lanes((32, 256)) // 8).astype(BF16)
    columns = (rows_of((80, 9)) // 8 == lanes((80, 9))).astype(BF16)
    wide = lax.dot_general(
        spread, dot(columns, w1[...]).astype(BF16), (((1,), (1,)), ((), ())), preferred_element_type=F32
    )
    same = rows_of((256, 80)) % 8 == lanes((256, 80)) % 8
    w1k[...] = jnp.where(same, wide, 0.0).astype(BF16)
    wide = dot(dot(spread, w2[...]).astype(BF16), spread_t)
    same = rows_of((256, 256)) % 8 == lanes((256, 256)) % 8
    w2k[...] = jnp.where(same, wide, 0.0).astype(BF16)
    wide = jnp.broadcast_to(dot(w3[...], spread_t), (16, 256))
    same = rows_of((16, 256)) == lanes((16, 256)) % 8
    w3k[...] = jnp.where(same, wide, 0.0).astype(BF16)
    mine = rows_of((256, 32)) // 8 == lanes((256, 32))
    for bias, kept in ((b1, b1k), (b2, b2k)):
        bias_column = jnp.sum(jnp.where(mine, bias[...], 0.0), axis=1, keepdims=True)
        kept[...] = jnp.broadcast_to(bias_column, (256, 128))
    lb2[...] = jnp.zeros_like(lb2)
    for p in range(28):
        for first in (0, 24):
            db[0, pl.ds(at0(p) + first, 8), :] = jnp.zeros((8, 128), F32)
    for c in vel_copies:
        c.wait_recv()
    for c in range(3):
        vb[c, column(-1), :] = ry[1, c]
        vb[c, column(16), :] = ry[2, c]

    more_copies = []
    for dx, dy, dz in EDGES:
        i, j, k = (1 - dx) // 2, (1 - dy) // 2, (1 - dz) // 2
        if dz == 0:
            src, dst = sxy.at[1 - i, 1 - j], rxy.at[i, j]
        elif dy == 0:
            src, dst = sz, rxz.at[k, i, pl.ds(0, 3)]
        else:
            part, rows = pl.ds(8 * (1 - j), 8), pl.ds(24 * j, 8)
            src, dst = sz.at[:, part, :], rz.at[k, pl.ds(0, 3), rows, :]
        more_copies.append(cp.start(src, dst, (dx, dy, dz)))
    more_copies += [
        cp.start(sy.at[2], ry.at[0], (0, 1, 0)),
        cp.start(sy.at[1], ry.at[3], (0, -1, 0)),
        cp.start(vel.at[:, 14], vb.at[:, pl.ds(at(-2), 16), :], (1, 0, 0)),
        cp.start(vel.at[:, 1], vb.at[:, pl.ds(at(17), 16), :], (-1, 0, 0)),
    ]

    for first_x in range(0, 16, 4):
        listing = [[] for _ in range(10)]
        for x in range(first_x, first_x + 4):
            base = at(x)
            g = []
            for c in range(3):
                plane = vb[c, pl.ds(base, 16), :]
                after = lane_roll(rz[1, c, pl.ds(8, 16), :], 125 - 8 * x)
                before = lane_roll(rz[0, c, pl.ds(8, 16), :], -(8 * x + 5))
                after = jnp.where(lane16 == 127, after, lane_roll(plane, -1))
                before = jnp.where(lane16 == 0, before, lane_roll(plane, 1))
                around = [
                    (vb[c, pl.ds(base + step, 16), :], vb[c, pl.ds(base - step, 16), :])
                    for step in (PLANE_ROWS, 1)
                ]
                g.append([0.5 * (a - b) for a, b in around + [(after, before)]])
            entries = [
                g[0][0], g[1][1], g[2][2],
                0.5 * (g[0][1] + g[1][0]), 0.5 * (g[0][2] + g[2][0]), 0.5 * (g[1][2] + g[2][1]),
                0.5 * (g[0][1] - g[1][0]), 0.5 * (g[0][2] - g[2][0]), 0.5 * (g[1][2] - g[2][1]),
                jnp.zeros((16, 128), F32),
            ]
            for tiles, entry in zip(listing, entries):
                tiles += [entry[0:8], entry[8:16]]
        features = jnp.concatenate(
            [jnp.concatenate(tiles, axis=1) for tiles in listing], axis=0
        ).astype(BF16)
        bias = jnp.concatenate([b1k[...]] * 8, axis=1)
        hidden = jnp.tanh(dot(w1k[...], features) + bias).astype(BF16)
        bias = jnp.concatenate([b2k[...]] * 8, axis=1)
        second = jnp.tanh(dot(w2k[...], hidden) + bias).astype(BF16)
        s = dot(w3k[...], second)[0:8]
        soft = GAIN * (jnp.maximum(s, 0.0) + jnp.log1p(jnp.exp(-jnp.abs(s))))
        for k in range(8):
            nb[pl.ds(at(first_x + k // 2, 8 * (k % 2)), 8), :] = soft[:, 128 * k : 128 * k + 128]

    for k, y in enumerate((0, 1, 14, 15)):
        syn[k] = nb[column(y), :]
    szn[...] = pack_z(lambda x: nb[pl.ds(at(x), 16), :])
    for i in (0, 1):
        for j in (0, 1):
            sxyn[i, j, pl.ds(0, 1), :] = nb[pl.ds(at(15 * i, 15 * j), 1), :]
    visc_copies = []
    for dx, dy, dz in EDGES:
        i, j, k = (1 - dx) // 2, (1 - dy) // 2, (1 - dz) // 2
        if dz == 0:
            src, dst = sxyn.at[1 - i, 1 - j], rxyn.at[i, j]
        elif dy == 0:
            src, dst = szn, rxz.at[k, i, 3]
        else:
            part, rows = pl.ds(8 * (1 - j), 8), pl.ds(24 * j, 8)
            src, dst = szn.at[part, :], rz.at[k, 3, rows, :]
        visc_copies.append(cp.start(src, dst, (dx, dy, dz)))
    visc_copies += [
        cp.start(szn, rz.at[0, 3, pl.ds(8, 16), :], (0, 0, 1)),
        cp.start(szn, rz.at[1, 3, pl.ds(8, 16), :], (0, 0, -1)),
        cp.start(syn.at[pl.ds(2, 2)], ryn.at[pl.ds(0, 2)], (0, 1, 0)),
        cp.start(syn.at[pl.ds(0, 2)], ryn.at[pl.ds(2, 2)], (0, -1, 0)),
    ]
    for x in (14, 15):
        here, there = pl.ds(at(x), 16), pl.ds(at(x - 16), 16)
        visc_copies.append(cp.start(nb.at[here, :], nb.at[there, :], (1, 0, 0)))
    for x in (0, 1):
        here, there = pl.ds(at(x), 16), pl.ds(at(x + 16), 16)
        visc_copies.append(cp.start(nb.at[here, :], nb.at[there, :], (-1, 0, 0)))

    slot = lanes((32, 128)) % 8

    def beyond(f, own):
        none = jnp.zeros((8, 128), F32)
        whole = jnp.concatenate([none, own, none], axis=0)
        outer = jnp.where(slot < 4, lane_roll(rz[0, f], -4), lane_roll(rz[1, f], 4))
        whole = jnp.where((slot >= 2) & (slot < 6), whole, outer)
        cz[f] = whole
        ends = jnp.where(slot == 0, lane_roll(whole, -1), lane_roll(whole, -5))
        for x in range(16):
            zb[f, pl.ds(at(x, -4), 24), :] = lane_roll(ends, -(8 * x + 1))[4:28]
        zb[f, pl.ds(at(-1), 16), :] = jnp.where(
            lane16 == 127, lane_roll(rxz[0, 0, f], 2), lane_roll(rxz[1, 0, f], 6)
        )
        zb[f, pl.ds(at(16), 16), :] = jnp.where(
            lane16 == 127, lane_roll(rxz[0, 1, f], 122), lane_roll(rxz[1, 1, f], -2)
        )

    for c in more_copies:
        c.wait_recv()
    for c in range(3):
        vb[c, column(-2), :] = ry[0, c]
        vb[c, column(17), :] = ry[3, c]
        for i in (0, 1):
            for j in (0, 1):
                vb[c, pl.ds(at(17 * i - 1, 17 * j - 1), 1), :] = rxy[i, j, pl.ds(c, 1), :]
        beyond(c, sz[c])
    for c in visc_copies:
        c.wait_recv()
    for k, y in enumerate((-2, -1, 16, 17)):
        nb[column(y), :] = ryn[k]
    for i in (0, 1):
        for j in (0, 1):
            nb[pl.ds(at(17 * i - 1, 17 * j - 1), 1), :] = rxyn[i, j, pl.ds(0, 1), :]
    beyond(3, szn[...])

    def change(i, n_mid, n_near, v_mid, v_near):
        total = 0.0
        for j in range(3):
            (up, down), (up_j, down_j) = v_near[i][j], v_near[j][j]
            total = total + 0.5 * (n_mid + n_near[j][0]) * (up - v_mid[i])
            total = total - 0.5 * (n_mid + n_near[j][1]) * (v_mid[i] - down)
            total = total - 0.5 * (up_j * up - down_j * down)
        return v_mid[i] + TIME_STEP * total

    def near(load, ends, start, n):
        mid = load(start)
        lane = lanes((n, 128))
        return mid, [
            (load(start + PLANE_ROWS), load(start - PLANE_ROWS)),
            (load(start + 1), load(start - 1)),
            (
                lane_roll(jnp.where(lane == 0, ends, mid), -1),
                lane_roll(jnp.where(lane == 127, ends, mid), 1),
            ),
        ]

    def tendency(start, n, components):
        where = pl.ds(start, n)
        n_mid, n_near = near(lambda r: nb[pl.ds(r, n), :], zb[3, where, :], start, n)
        both = [near(lambda r, c=c: vb[c, pl.ds(r, n), :], zb[c, where, :], start, n) for c in range(3)]
        for i in components:
            pb[i, where, :] = change(i, n_mid, n_near, [b[0] for b in both], [b[1] for b in both])

    for x in range(16):
        tendency(at(x), 16, (0, 1, 2))
    tendency(at(-1), 16, (0,))
    tendency(at(16), 16, (0,))
    for x in range(-1, 16):
        tendency(at(x, 16), 8, (1,))

    def near_end(f):
        mid = cz[f, pl.ds(8, 16), :]
        above = jnp.where(lane16 == 126, lane_roll(rxz[1, 1, f], 124), lane_roll(rxz[0, 1, f], 116))
        below = jnp.where(lane16 == 6, lane_roll(rxz[1, 0, f], 12), lane_roll(rxz[0, 0, f], 4))
        return mid, [
            (
                jnp.where(lane16 >= 120, above, lane_roll(mid, -8)),
                jnp.where(lane16 < 8, below, lane_roll(mid, 8)),
            ),
            (cz[f, pl.ds(9, 16), :], cz[f, pl.ds(7, 16), :]),
            (lane_roll(mid, -1), lane_roll(mid, 1)),
        ]

    fields = [near_end(f) for f in range(4)]
    far = change(2, *fields[3], [f[0] for f in fields[:3]], [f[1] for f in fields[:3]])
    far = jnp.where(lane16 % 8 == 0, lane_roll(far, -1), lane_roll(far, -5))

    for x in range(16):
        base = at(x)
        plane, ends = pb[2, pl.ds(base, 16), :], lane_roll(far, -(8 * x + 1))
        total = pb[0, pl.ds(base + PLANE_ROWS, 16), :] - pb[0, pl.ds(base - PLANE_ROWS, 16), :]
        total = total + pb[1, pl.ds(base + 1, 16), :] - pb[1, pl.ds(base - 1, 16), :]
        total = total + lane_roll(jnp.where(lane16 == 0, ends, plane), -1)
        dv[x] = 0.5 * (total - lane_roll(jnp.where(lane16 == 127, ends, plane), 1))
        dvr[pl.ds(16 * x, 16), :] = dv[x]

    for half in range(2):
        packed = jnp.zeros((16, 128), F32)
        for k in range(8):
            packed = jnp.where(lane16 // 16 == k, lane_roll(dv[8 * half + k], 16 * k + 8), packed)
        sdz[half] = packed
    for y in range(6):
        for j, first in enumerate((0, 10)):
            sdy[j, y] = dvr[pl.ds(first + y, 16, stride=16), :]
    for i, j, k, (a, b) in CORNER:
        x, y = (15 - a if i else a), (15 - b if j else b)
        sde[i, j, pl.ds(k, 1), :] = dvr[pl.ds(16 * x + y, 1), :]
    div_copies = []
    for dx, dy, dz in AROUND:
        here_x, here_y = (1 - dx) // 2, (1 - dy) // 2
        if dz == 0:
            if dy == 0:
                src, dst = dv.at[pl.ds(10 if dx > 0 else 0, 6)], rdx.at[here_x]
            elif dx == 0:
                src, dst = sdy.at[1 - here_y], rdy.at[here_y]
            else:
                src, dst = sde.at[1 - here_x, 1 - here_y], rde.at[here_x, here_y]
        else:
            half = pl.ds(0, 2) if dx == 0 else pl.ds(1 if dx > 0 else 0, 1)
            slot = pl.ds(1, 2) if dx == 0 else pl.ds(0 if dx > 0 else 3, 1)
            part = pl.ds(0, 16) if dy == 0 else pl.ds(8 if dy > 0 else 0, 8)
            rows = pl.ds(8, 16) if dy == 0 else pl.ds(0 if dy > 0 else 24, 8)
            src, dst = sdz.at[half, part, :], rdz.at[(1 - dz) // 2, slot, rows, :]
        div_copies.append(cp.start(src, dst, (dx, dy, dz)))

    for x in range(16):
        db[0, pl.ds(at0(x + 6) + 8, 16), :] = dv[x]
    for c in div_copies:
        c.wait_recv()
    for x in range(6):
        for side, p in ((0, x), (1, 22 + x)):
            db[0, pl.ds(at0(p) + 8, 16), :] = rdx[side, x]
    for i, j, k, (a, b) in CORNER:
        p, y = (22 + a if i else 5 - a), (16 + b if j else -1 - b)
        db[0, pl.ds(at0(p) + 8 + y, 1), :] = rde[i, j, pl.ds(k, 1), :]
    for y in range(6):
        db[0, pl.ds(at0(6) + 2 + y, 16, stride=32), :] = rdy[0, y]
        db[0, pl.ds(at0(6) + 24 + y, 16, stride=32), :] = rdy[1, y]
    lane32 = lanes((32, 128))
    for g in range(4):
        both = jnp.where(lane32 % 16 < 8, rdz[0, g], rdz[1, g])
        for k in range(8):
            x = 8 * (g - 1) + k
            if -6 <= x < 22:
                db[1, pl.ds(at0(x + 6), 32), :] = lane_roll(both, -(16 * k + 8))

    for p in range(1, 27, 2):
        b, around = sum6_wide(db, at0(p), 64, 32)
        for t in (0, 1):
            v0[t, pl.ds(at0(p), 64), :] = -C * (1.2 * b[t] + C * around[t])
    for k in range(12):
        for edge in (0, 24):
            rs[pl.ds(32 * k + edge, 8), :] = jnp.zeros((8, 256), F32)
        pair = [0.0, 0.0]
        for base in (at0(2 + 2 * k) + 4, at0(3 + 2 * k) + 4):
            v, around = sum6_wide(v0, base, 24, 32)
            for t in (0, 1):
                pair[t] = pair[t] + db[t, pl.ds(base, 24), :] - (around[t] - 6.0 * v[t])
        for t in (0, 1):
            rs[pl.ds(32 * k + 4, 24), pl.ds(128 * t, 128)] = pair[t]
    halve = jnp.where(coarse_lane((256, 128), 0) == lanes((256, 128)), 0.125, 0.0).astype(F32)
    rt[...] = exact_dot(rs[...], halve)
    s1[...] = rt[pl.ds(0, 192, stride=2), :] + rt[pl.ds(1, 192, stride=2), :]

    lane8 = lanes((8, 128))
    packed = jnp.zeros((8, 128), F32)
    for x in range(8):
        plane = s1[pl.ds(16 * (x + 2) + 4, 8), :]
        r1c[x] = plane
        packed = jnp.where(lane8 // 8 == 2 * x, lane_roll(plane, 16 * x - 88), packed)
        packed = jnp.where(lane8 // 8 == 2 * x + 1, lane_roll(plane, 16 * x + 8 - 32), packed)
    sez[...] = packed

    for p in range(1, 11, 5):
        b, around = sum6(s1, 16 * p, 80, 16)
        v1s[pl.ds(16 * p, 80), :] = -4.0 * C * (1.2 * b + C * around)
    parts = []
    for k in range(4):
        base = 16 * (2 + 2 * k)
        v, around = sum6(v1s, base, 32, 16)
        residual = s1[pl.ds(base, 32), :] - 0.25 * (around - 6.0 * v)
        parts.append(residual[0:16] + residual[16:32])
    halve = halve[0:128]
    rt[pl.ds(0, 64), :] = exact_dot(jnp.concatenate(parts, axis=0), halve)
    packed = jnp.zeros((8, 128), F32)
    for x in range(4):
        plane = rt[pl.ds(16 * x, 8, stride=2), :] + rt[pl.ds(16 * x + 1, 8, stride=2), :]
        packed = jnp.where(lane8 // 32 == x, lane_roll(plane, 32 * x - 48), packed)
    sa[...] = packed
    ra[3, 1] = packed
    yz_copies = [
        cp.start(sa, ra.at[3 - dy, 1 - dz], (0, dy, dz))
        for dy in (3, -3, 2, -2, 1, -1, 0)
        for dz in (1, -1, 0)
        if (dy, dz) != (0, 0)
    ]
    src_copies = []
    for dx, dy, dz in AROUND:
        here_x, here_y = (1 - dx) // 2, (1 - dy) // 2
        if dz == 0:
            planes = pl.ds(3 if dx > 0 else 0, 5)
            if dy == 0:
                src, dst = r1c.at[planes], rex.at[here_x]
            elif dx == 0:
                src, dst = r1c, rey.at[here_y]
            else:
                src, dst = r1c.at[planes], ree.at[here_x, here_y]
        else:
            src, dst = sez, rez.at[(1 - dz) // 2, 1 - dx, pl.ds(8 * (1 - dy), 8), :]
        src_copies.append(cp.start(src, dst, (dx, dy, dz)))

    for c in yz_copies:
        c.wait_recv()
    for dy in range(7):
        for x in range(4):
            before, here, after = (
                lane_roll(ra[dy, k], lane - 32 * x) for k, lane in ((0, 16), (1, 48), (2, 80))
            )
            whole = jnp.where(lane8 < 48, before, jnp.where(lane8 < 80, here, after))
            lb2[pl.ds(32 * (12 + x) + 4 * dy, 4), :] = whole[2:6]
    lane32 = lanes((32, 128))
    for k in range(2):
        left, right = lb2[pl.ds(32 * (12 + 2 * k), 32), :], lb2[pl.ds(32 * (13 + 2 * k), 32), :]
        sb[k] = jnp.where(lane32 < 64, lane_roll(left, -32), lane_roll(right, 32))
    x_copies = []
    for dx in (3, -3, 2, -2, 1, -1):
        rows = pl.ds(0, 24 if abs(dx) == 3 else 32)
        x_copies.append(cp.start(sb.at[:, rows, :], rb.at[3 - dx, :, rows, :], (dx, 0, 0)))

    for c in src_copies:
        c.wait_recv()
    lane24 = lanes((24, 128))
    for p in range(18):
        dx, x = (p - 5) // 8, (p - 5) % 8
        if dx == 0:
            three = [rey[0, x], r1c[x], rey[1, x]]
        else:
            side = (dx + 1) // 2
            k = x - 3 if dx < 0 else x
            three = [ree[side, 0, k], rex[side, k], ree[side, 1, k]]
        before = lane_roll(rez[0, dx + 1], 24 - 16 * x)
        after = lane_roll(rez[1, dx + 1], 96 - 16 * x - 8)
        here = jnp.concatenate(three, axis=0)
        lb1[pl.ds(24 * p, 24), :] = jnp.where(
            lane24 < 32, before, jnp.where(lane24 < 96, here, after)
        )
    for p in range(1, 17, 4):
        b, around = sum6(lb1, 24 * p, 96, 24)
        v1[pl.ds(24 * p, 96), :] = -4.0 * C * (1.2 * b + C * around)

    cp.sent()
    for c in x_copies:
        c.wait_recv()
    for dx in (-3, -2, -1, 1, 2, 3):
        n = 24 if abs(dx) == 3 else 32
        for x in range(4):
            plane = lane_roll(rb[3 + dx, x // 2, pl.ds(0, n), :], 32 if x % 2 == 0 else -32)
            lb2[pl.ds(32 * (4 * (3 + dx) + x), n), :] = plane

    for p in range(1, 27, 2):
        b, around = sum6(lb2, 32 * p, 64, 32)
        v2[pl.ds(32 * p, 64), :] = -16.0 * C * (1.2 * b + C * around)
    for k in range(12):
        base = 32 * (2 + 2 * k)
        v, around = sum6(v2, base, 64, 32)
        residual = lb2[pl.ds(base, 64), :] - 0.0625 * (around - 6.0 * v)
        rs[pl.ds(32 * k, 32), pl.ds(0, 128)] = residual[0:32] + residual[32:64]
    rt[...] = exact_dot(rs[:, 0:128], halve)
    lb3[...] = rt[pl.ds(0, 192, stride=2), :] + rt[pl.ds(1, 192, stride=2), :]

    b, around = sum6(lb3, 16, 160, 16)
    v3[pl.ds(16, 160), :] = -64.0 * C * (1.2 * b + C * around)
    v, around = sum6(v3, 32, 128, 16)
    u3[pl.ds(32, 128), :] = 0.2 * v + C * around - 64.0 * C * lb3[pl.ds(32, 128), :]
    v, around = sum6(u3, 48, 96, 16)
    coarse = 0.2 * v + C * around - 64.0 * C * lb3[pl.ds(48, 96), :]

    double = jnp.where(rows_of((128, 256)) == coarse_lane((128, 256), 1), 1.0, 0.0).astype(F32)
    fine = exact_dot(coarse, double[:, 0:128])
    for k in range(6):
        for p in (8 + 2 * k, 9 + 2 * k):
            for odd in (0, 1):
                where = pl.ds(32 * p + odd, 16, stride=2)
                v2[where, :] = v2[where, :] + fine[16 * k : 16 * k + 16]
    for p in range(9, 19, 2):
        v, around = sum6(v2, 32 * p, 64, 32)
        u2[pl.ds(32 * p, 64), :] = 0.2 * v + C * around - 16.0 * C * lb2[pl.ds(32 * p, 64), :]
    for k in range(4):
        base = 32 * (10 + 2 * k)
        v, around = sum6(u2, base, 64, 32)
        rs[pl.ds(64 * k, 64), pl.ds(0, 128)] = (
            0.2 * v + C * around - 16.0 * C * lb2[pl.ds(base, 64), :]
        )

    fine = exact_dot(rs[0:256, 0:128], double[:, 0:128])
    for k in range(8):
        for p in (1 + 2 * k, 2 + 2 * k):
            for odd in (0, 1):
                where = pl.ds(24 * p + odd, 12, stride=2)
                v1[where, :] = v1[where, :] + fine[32 * k + 8 : 32 * k + 20]
    for p in range(2, 16, 2):
        v, around = sum6(v1, 24 * p, 48, 24)
        u1[pl.ds(24 * p, 48), :] = 0.2 * v + C * around - 4.0 * C * lb1[pl.ds(24 * p, 48), :]
    for k in range(6):
        base = 24 * (3 + 2 * k)
        v, around = sum6(u1, base, 48, 24)
        rs[pl.ds(48 * k, 48), pl.ds(0, 128)] = (
            0.2 * v + C * around - 4.0 * C * lb1[pl.ds(base, 48), :]
        )

    for t in (0, 1):
        fine = exact_dot(rs[0:288, 0:128], double[:, 128 * t : 128 * t + 128])
        for k in range(12):
            for p in (2 + 2 * k, 3 + 2 * k):
                for odd in (0, 1):
                    where = pl.ds(at0(p) + odd, 16, stride=2)
                    v0[t, where, :] = v0[t, where, :] + fine[24 * k + 4 : 24 * k + 20]
    for p in range(4, 24):
        base = at0(p) + 4
        v, around = sum6_wide(v0, base, 24, 32)
        for t in (0, 1):
            b = db[t, pl.ds(base, 24), :]
            u0[t, pl.ds(base, 24), :] = 0.2 * v[t] + C * around[t] - C * b
    for p in range(5, 23):
        base = at0(p) + 4
        v, around = sum6_wide(u0, base, 24, 32)
        for t in (0, 1):
            b = db[t, pl.ds(base, 24), :]
            v0[t, pl.ds(base, 24), :] = 0.2 * v[t] + C * around[t] - C * b

    for x in range(16):
        base = at0(x + 6) + 8
        here, beyond = v0[0, pl.ds(base, 16), :], v0[1, pl.ds(base, 16), :]
        pout[x] = here
        slopes = [
            v0[0, pl.ds(base + 32, 16), :] - v0[0, pl.ds(base - 32, 16), :],
            v0[0, pl.ds(base + 1, 16), :] - v0[0, pl.ds(base - 1, 16), :],
            jnp.where(lane16 == 127, lane_roll(beyond, -1), lane_roll(here, -1))
            - jnp.where(lane16 == 0, lane_roll(beyond, 1), lane_roll(here, 1)),
        ]
        for c in range(3):
            vout[c, x] = pb[c, pl.ds(at(x), 16), :] - 0.5 * slopes[c]


def body(velocity, input_weight, input_bias, hidden_weight, hidden_bias, output_weight):
    def scratch(*shape):
        return pltpu.VMEM(shape, F32)

    plane_buffer = 16 + PLANE_ROWS * 20
    level0 = 16 + 32 * 28
    return pl.pallas_call(
        kernel,
        out_shape=(
            pltpu.VMEM((3, 16, 16, 128), F32),
            pltpu.VMEM((16, 16, 128), F32),
        ),
        in_specs=[pl.BlockSpec(memory_space=pltpu.HBM)] * 6,
        out_specs=[pl.BlockSpec(memory_space=pltpu.VMEM)] * 2,
        scratch_shapes=[
            scratch(3, 16, 16, 128),
            pltpu.VMEM((9, 32), BF16),
            scratch(1, 32),
            pltpu.VMEM((32, 32), BF16),
            scratch(1, 32),
            pltpu.VMEM((1, 32), BF16),
            pltpu.VMEM((256, 80), BF16),
            pltpu.VMEM((256, 256), BF16),
            pltpu.VMEM((16, 256), BF16),
            scratch(256, 128),
            scratch(256, 128),
            scratch(3, plane_buffer, 128),
            scratch(plane_buffer, 128),
            scratch(3, plane_buffer, 128),
            scratch(4, 3, 16, 128),
            scratch(3, 16, 128),
            scratch(2, 2, 8, 128),
            scratch(4, 3, 16, 128),
            scratch(2, 4, 32, 128),
            scratch(2, 2, 8, 128),
            scratch(2, 2, 4, 16, 128),
            scratch(4, 16, 128),
            scratch(16, 128),
            scratch(2, 2, 8, 128),
            scratch(4, 16, 128),
            scratch(2, 2, 8, 128),
            scratch(4, 32, 128),
            scratch(4, plane_buffer, 128),
            scratch(16, 16, 128),
            scratch(256, 128),
            scratch(2, 6, 16, 128),
            scratch(2, 2, 16, 128),
            scratch(2, 16, 128),
            scratch(2, 6, 16, 128),
            scratch(2, 6, 16, 128),
            scratch(2, 2, 16, 128),
            scratch(2, 4, 32, 128),
            scratch(2, level0, 128),
            scratch(2, level0, 128),
            scratch(2, level0, 128),
            scratch(384, 256),
            scratch(384, 128),
            scratch(192, 128),
            scratch(192, 128),
            scratch(8, 8, 128),
            scratch(8, 128),
            scratch(2, 5, 8, 128),
            scratch(2, 8, 8, 128),
            scratch(2, 2, 5, 8, 128),
            scratch(2, 3, 24, 128),
            scratch(432, 128),
            scratch(432, 128),
            scratch(432, 128),
            scratch(8, 128),
            scratch(7, 3, 8, 128),
            scratch(2, 32, 128),
            scratch(7, 2, 32, 128),
            scratch(896, 128),
            scratch(896, 128),
            scratch(896, 128),
            scratch(192, 128),
            scratch(192, 128),
            scratch(192, 128),
            pltpu.SemaphoreType.DMA((N_COPIES,)),
            pltpu.SemaphoreType.DMA((N_COPIES,)),
            pltpu.SemaphoreType.DMA((6,)),
        ],
        compiler_params=pltpu.CompilerParams(
            collective_id=0, has_side_effects=True, vmem_limit_bytes=60 * 1024 * 1024
        ),
    )(
        velocity,
        input_weight.T,
        input_bias.reshape(1, 32),
        hidden_weight,
        hidden_bias.reshape(1, 32),
        output_weight.reshape(1, 32),
    )


def solution(mesh):
    return jax.shard_map(
        body,
        mesh=mesh,
        in_specs=(P(None, "gx", "gy", "gz"), P(), P(), P(), P(), P()),
        out_specs=(P(None, "gx", "gy", "gz"), P("gx", "gy", "gz")),
        check_vma=False,
    )
```

time: 49.9 us -> 47.2 us (0.946)
  Pallas kernels: 47.7 us -> 45 us
    pallas_call x1, Pallas kernels: 47.7 us -> 45 us  [body(): pl.pallas_call(kernel, out_shape=(pltpu.VMEM((3, 16, 16, 128), F32), pltp...]
where the time goes in v3:
time: 47.2 us; the launch traced here: 47.1 us
  Pallas kernels  45 us (95%)
  local copies, waits for them, and re-layouts  1.4 us (3%)
  between operations  0.64 us (1%)
    pallas_call x1, Pallas kernels, body(): pl.pallas_call(kernel, out_shape=(pltpu.VMEM((3, 16, 16, 128), F32), pltp...  45 us
    unnamed x2, local copies, waits for them, and re-layouts  1.4 us

profile of v3, /device:TPU:1, one launch (start us, length us, event | category | flops | bytes accessed | tf_op | source)
XLA Modules:
  0.0 47.1 jit_solution(3646863880002258814)
XLA Ops:
  0.6 45.0 %shard_map.77 = (f32[3,16,16,128]{3,2,1,0:T(8,128)S(1)}, f32[16,16,128]{2,1,0:T(8,128)S(1)}) custom-call(f32[3,16,16,128]{3,2,1,0:T(8,128)} %vel_in.1, bf16[9,32]{1,0:T(8,128)(2,1)} %bitcast.4, f32[1,32]{1,0:T(1,128)} %bitcast.5, bf16[32,32]{1,0:T(8,128)(2,1)} %w2_in.1, f32[1,32]{1,0:T(1,128)} %bitcast.6, bf16[1,32]{1,0:T(2,128)(2,1)} %bitcast.7), custom_call_target="tpu_custom_call" | custom-call | tf_op jit(solution)/shard_map/pallas_call | solution.py:641
  45.7 0.7 %copy.10 = f32[3,16,16,128]{3,2,1,0:T(8,128)} copy(f32[3,16,16,128]{3,2,1,0:T(8,128)S(1)} %get-tuple-element.2) | data formatting | bytes 786432
  46.4 0.7 %copy.11 = f32[16,16,128]{2,1,0:T(8,128)} copy(f32[16,16,128]{2,1,0:T(8,128)S(1)} %get-tuple-element.3) | data formatting | bytes 262144

commit v4 on v3

--- a/solution.py
+++ b/solution.py
@@ -203,27 +203,9 @@
         vb[c, column(-1), :] = ry[1, c]
         vb[c, column(16), :] = ry[2, c]
 
-    more_copies = []
-    for dx, dy, dz in EDGES:
-        i, j, k = (1 - dx) // 2, (1 - dy) // 2, (1 - dz) // 2
-        if dz == 0:
-            src, dst = sxy.at[1 - i, 1 - j], rxy.at[i, j]
-        elif dy == 0:
-            src, dst = sz, rxz.at[k, i, pl.ds(0, 3)]
-        else:
-            part, rows = pl.ds(8 * (1 - j), 8), pl.ds(24 * j, 8)
-            src, dst = sz.at[:, part, :], rz.at[k, pl.ds(0, 3), rows, :]
-        more_copies.append(cp.start(src, dst, (dx, dy, dz)))
-    more_copies += [
-        cp.start(sy.at[2], ry.at[0], (0, 1, 0)),
-        cp.start(sy.at[1], ry.at[3], (0, -1, 0)),
-        cp.start(vel.at[:, 14], vb.at[:, pl.ds(at(-2), 16), :], (1, 0, 0)),
-        cp.start(vel.at[:, 1], vb.at[:, pl.ds(at(17), 16), :], (-1, 0, 0)),
-    ]
-
-    for first_x in range(0, 16, 4):
+    for first_x in range(0, 16, 8):
         listing = [[] for _ in range(10)]
-        for x in range(first_x, first_x + 4):
+        for x in range(first_x, first_x + 8):
             base = at(x)
             g = []
             for c in range(3):
@@ -248,13 +230,31 @@
         features = jnp.concatenate(
             [jnp.concatenate(tiles, axis=1) for tiles in listing], axis=0
         ).astype(BF16)
-        bias = jnp.concatenate([b1k[...]] * 8, axis=1)
+        if first_x == 0:
+            more_copies = []
+            for dx, dy, dz in EDGES:
+                i, j, k = (1 - dx) // 2, (1 - dy) // 2, (1 - dz) // 2
+                if dz == 0:
+                    src, dst = sxy.at[1 - i, 1 - j], rxy.at[i, j]
+                elif dy == 0:
+                    src, dst = sz, rxz.at[k, i, pl.ds(0, 3)]
+                else:
+                    part, rows = pl.ds(8 * (1 - j), 8), pl.ds(24 * j, 8)
+                    src, dst = sz.at[:, part, :], rz.at[k, pl.ds(0, 3), rows, :]
+                more_copies.append(cp.start(src, dst, (dx, dy, dz)))
+            more_copies += [
+                cp.start(sy.at[2], ry.at[0], (0, 1, 0)),
+                cp.start(sy.at[1], ry.at[3], (0, -1, 0)),
+                cp.start(vel.at[:, 14], vb.at[:, pl.ds(at(-2), 16), :], (1, 0, 0)),
+                cp.start(vel.at[:, 1], vb.at[:, pl.ds(at(17), 16), :], (-1, 0, 0)),
+            ]
+        bias = jnp.concatenate([b1k[...]] * 16, axis=1)
         hidden = jnp.tanh(dot(w1k[...], features) + bias).astype(BF16)
-        bias = jnp.concatenate([b2k[...]] * 8, axis=1)
+        bias = jnp.concatenate([b2k[...]] * 16, axis=1)
         second = jnp.tanh(dot(w2k[...], hidden) + bias).astype(BF16)
         s = dot(w3k[...], second)[0:8]
         soft = GAIN * (jnp.maximum(s, 0.0) + jnp.log1p(jnp.exp(-jnp.abs(s))))
-        for k in range(8):
+        for k in range(16):
             nb[pl.ds(at(first_x + k // 2, 8 * (k % 2)), 8), :] = soft[:, 128 * k : 128 * k + 128]
 
     for k, y in enumerate((0, 1, 14, 15)):
@@ -476,8 +476,8 @@
     for x in range(4):
         plane = rt[pl.ds(16 * x, 8, stride=2), :] + rt[pl.ds(16 * x + 1, 8, stride=2), :]
         packed = jnp.where(lane8 // 32 == x, lane_roll(plane, 32 * x - 48), packed)
-    sa[...] = packed
-    ra[3, 1] = packed
+    sa[...] = packed[2:6]
+    ra[3, 1] = packed[2:6]
     yz_copies = [
         cp.start(sa, ra.at[3 - dy, 1 - dz], (0, dy, dz))
         for dy in (3, -3, 2, -2, 1, -1, 0)
@@ -501,13 +501,14 @@
 
     for c in yz_copies:
         c.wait_recv()
+    lane4 = lanes((4, 128))
     for dy in range(7):
         for x in range(4):
             before, here, after = (
                 lane_roll(ra[dy, k], lane - 32 * x) for k, lane in ((0, 16), (1, 48), (2, 80))
             )
-            whole = jnp.where(lane8 < 48, before, jnp.where(lane8 < 80, here, after))
-            lb2[pl.ds(32 * (12 + x) + 4 * dy, 4), :] = whole[2:6]
+            whole = jnp.where(lane4 < 48, before, jnp.where(lane4 < 80, here, after))
+            lb2[pl.ds(32 * (12 + x) + 4 * dy, 4), :] = whole
     lane32 = lanes((32, 128))
     for k in range(2):
         left, right = lb2[pl.ds(32 * (12 + 2 * k), 32), :], lb2[pl.ds(32 * (13 + 2 * k), 32), :]
@@ -632,13 +633,22 @@
             vout[c, x] = pb[c, pl.ds(at(x), 16), :] - 0.5 * slopes[c]
 
 
+def hand_over(velocity, pressure, velocity_out, pressure_out, sem):
+    first = pltpu.make_async_copy(velocity, velocity_out, sem.at[0])
+    second = pltpu.make_async_copy(pressure, pressure_out, sem.at[1])
+    first.start()
+    second.start()
+    first.wait()
+    second.wait()
+
+
 def body(velocity, input_weight, input_bias, hidden_weight, hidden_bias, output_weight):
     def scratch(*shape):
         return pltpu.VMEM(shape, F32)
 
     plane_buffer = 16 + PLANE_ROWS * 20
     level0 = 16 + 32 * 28
-    return pl.pallas_call(
+    results = pl.pallas_call(
         kernel,
         out_shape=(
             pltpu.VMEM((3, 16, 16, 128), F32),
@@ -700,8 +710,8 @@
             scratch(432, 128),
             scratch(432, 128),
             scratch(432, 128),
-            scratch(8, 128),
-            scratch(7, 3, 8, 128),
+            scratch(4, 128),
+            scratch(7, 3, 4, 128),
             scratch(2, 32, 128),
             scratch(7, 2, 32, 128),
             scratch(896, 128),
@@ -725,6 +735,17 @@
         hidden_bias.reshape(1, 32),
         output_weight.reshape(1, 32),
     )
+    return pl.pallas_call(
+        hand_over,
+        out_shape=(
+            jax.ShapeDtypeStruct((3, 16, 16, 128), F32),
+            jax.ShapeDtypeStruct((16, 16, 128), F32),
+        ),
+        in_specs=[pl.BlockSpec(memory_space=pl.ANY)] * 2,
+        out_specs=[pl.BlockSpec(memory_space=pl.ANY)] * 2,
+        scratch_shapes=[pltpu.SemaphoreType.DMA((2,))],
+        compiler_params=pltpu.CompilerParams(vmem_limit_bytes=1024 * 1024),
+    )(*results)
 
 
 def solution(mesh):

time: 47.2 us -> 45.8 us (0.970)
  local copies, waits for them, and re-layouts: 1.4 us -> 0 us
    unnamed x2 -> x0, local copies, waits for them, and re-layouts: 1.4 us -> none
    pallas_call x0 -> x1, Pallas kernels: none -> 0.8 us  [body(): pl.pallas_call(hand_over, out_shape=(jax.ShapeDtypeStruct((3, 16, 16, 128...]
    pallas_call x1, Pallas kernels: 45 us -> 44.3 us  [body(): pl.pallas_call(kernel, out_shape=(pltpu.VMEM((3, 16, 16, 128), F32), pltp...]
where the time goes in v4:
time: 45.8 us; the launch traced here: 45.7 us
  Pallas kernels  45.1 us (98%)
  between operations  0.64 us (1%)
    pallas_call x1, Pallas kernels, body(): pl.pallas_call(kernel, out_shape=(pltpu.VMEM((3, 16, 16, 128), F32), pltp...  44.3 us

profile of v4, /device:TPU:1, one launch (start us, length us, event | category | flops | bytes accessed | tf_op | source)
XLA Modules:
  0.0 45.7 jit_solution(13439758504310739676)
XLA Ops:
  0.6 44.3 %shard_map.77 = (f32[3,16,16,128]{3,2,1,0:T(8,128)S(1)}, f32[16,16,128]{2,1,0:T(8,128)S(1)}) custom-call(f32[3,16,16,128]{3,2,1,0:T(8,128)} %vel_in.1, bf16[9,32]{1,0:T(8,128)(2,1)} %bitcast.4, f32[1,32]{1,0:T(1,128)} %bitcast.5, bf16[32,32]{1,0:T(8,128)(2,1)} %w2_in.1, f32[1,32]{1,0:T(1,128)} %bitcast.6, bf16[1,32]{1,0:T(2,128)(2,1)} %bitcast.7), custom_call_target="tpu_custom_call" | custom-call | tf_op jit(solution)/shard_map/pallas_call | solution.py:651
  44.9 0.8 %shard_map.78 = (f32[3,16,16,128]{3,2,1,0:T(8,128)}, f32[16,16,128]{2,1,0:T(8,128)}) custom-call(f32[3,16,16,128]{3,2,1,0:T(8,128)S(1)} %get-tuple-element.4.velocity, f32[16,16,128]{2,1,0:T(8,128)S(1)} %get-tuple-element.5.pressure), custom_call_target="tpu_custom_call" | custom-call | tf_op jit(solution)/shard_map/pallas_call | solution.py:738

commit v5 on v4

--- a/solution.py
+++ b/solution.py
@@ -573,39 +573,40 @@
             for odd in (0, 1):
                 where = pl.ds(32 * p + odd, 16, stride=2)
                 v2[where, :] = v2[where, :] + fine[16 * k : 16 * k + 16]
-    for p in range(9, 19, 2):
-        v, around = sum6(v2, 32 * p, 64, 32)
-        u2[pl.ds(32 * p, 64), :] = 0.2 * v + C * around - 16.0 * C * lb2[pl.ds(32 * p, 64), :]
-    for k in range(4):
-        base = 32 * (10 + 2 * k)
-        v, around = sum6(u2, base, 64, 32)
-        rs[pl.ds(64 * k, 64), pl.ds(0, 128)] = (
-            0.2 * v + C * around - 16.0 * C * lb2[pl.ds(base, 64), :]
+    for p in range(9, 19):
+        where = pl.ds(32 * p + 8, 16)
+        v, around = sum6(v2, 32 * p + 8, 16, 32)
+        u2[where, :] = 0.2 * v + C * around - 16.0 * C * lb2[where, :]
+    for k in range(8):
+        base = 32 * (10 + k) + 8
+        v, around = sum6(u2, base, 16, 32)
+        rs[pl.ds(16 * k, 16), pl.ds(0, 128)] = (
+            0.2 * v + C * around - 16.0 * C * lb2[pl.ds(base, 16), :]
         )
 
-    fine = exact_dot(rs[0:256, 0:128], double[:, 0:128])
+    fine = exact_dot(rs[0:128, 0:128], double[:, 0:128])
     for k in range(8):
         for p in (1 + 2 * k, 2 + 2 * k):
             for odd in (0, 1):
                 where = pl.ds(24 * p + odd, 12, stride=2)
-                v1[where, :] = v1[where, :] + fine[32 * k + 8 : 32 * k + 20]
+                v1[where, :] = v1[where, :] + fine[16 * k : 16 * k + 12]
     for p in range(2, 16, 2):
         v, around = sum6(v1, 24 * p, 48, 24)
         u1[pl.ds(24 * p, 48), :] = 0.2 * v + C * around - 4.0 * C * lb1[pl.ds(24 * p, 48), :]
-    for k in range(6):
-        base = 24 * (3 + 2 * k)
-        v, around = sum6(u1, base, 48, 24)
-        rs[pl.ds(48 * k, 48), pl.ds(0, 128)] = (
-            0.2 * v + C * around - 4.0 * C * lb1[pl.ds(base, 48), :]
+    for k in range(12):
+        base = 24 * (3 + k) + 4
+        v, around = sum6(u1, base, 16, 24)
+        rs[pl.ds(16 * k, 16), pl.ds(0, 128)] = (
+            0.2 * v + C * around - 4.0 * C * lb1[pl.ds(base, 16), :]
         )
 
     for t in (0, 1):
-        fine = exact_dot(rs[0:288, 0:128], double[:, 128 * t : 128 * t + 128])
+        fine = exact_dot(rs[0:192, 0:128], double[:, 128 * t : 128 * t + 128])
         for k in range(12):
             for p in (2 + 2 * k, 3 + 2 * k):
                 for odd in (0, 1):
                     where = pl.ds(at0(p) + odd, 16, stride=2)
-                    v0[t, where, :] = v0[t, where, :] + fine[24 * k + 4 : 24 * k + 20]
+                    v0[t, where, :] = v0[t, where, :] + fine[16 * k : 16 * k + 16]
     for p in range(4, 24):
         base = at0(p) + 4
         v, around = sum6_wide(v0, base, 24, 32)

time: 45.8 us -> 45.8 us (level)
  no operation moved by 1% of the time
where the time goes in v5:
time: 45.8 us; the launch traced here: 45.6 us
  Pallas kernels  45 us (98%)
  between operations  0.64 us (1%)
    pallas_call x1, Pallas kernels, body(): pl.pallas_call(kernel, out_shape=(pltpu.VMEM((3, 16, 16, 128), F32), pltp...  44.2 us

profile of v5, /device:TPU:1, one launch (start us, length us, event | category | flops | bytes accessed | tf_op | source)
XLA Modules:
  0.0 45.6 jit_solution(13811327723021100288)
XLA Ops:
  0.6 44.2 %shard_map.77 = (f32[3,16,16,128]{3,2,1,0:T(8,128)S(1)}, f32[16,16,128]{2,1,0:T(8,128)S(1)}) custom-call(f32[3,16,16,128]{3,2,1,0:T(8,128)} %vel_in.1, bf16[9,32]{1,0:T(8,128)(2,1)} %bitcast.4, f32[1,32]{1,0:T(1,128)} %bitcast.5, bf16[32,32]{1,0:T(8,128)(2,1)} %w2_in.1, f32[1,32]{1,0:T(1,128)} %bitcast.6, bf16[1,32]{1,0:T(2,128)(2,1)} %bitcast.7), custom_call_target="tpu_custom_call" | custom-call | tf_op jit(solution)/shard_map/pallas_call | solution.py:652
  44.8 0.8 %shard_map.78 = (f32[3,16,16,128]{3,2,1,0:T(8,128)}, f32[16,16,128]{2,1,0:T(8,128)}) custom-call(f32[3,16,16,128]{3,2,1,0:T(8,128)S(1)} %get-tuple-element.4.velocity, f32[16,16,128]{2,1,0:T(8,128)S(1)} %get-tuple-element.5.pressure), custom_call_target="tpu_custom_call" | custom-call | tf_op jit(solution)/shard_map/pallas_call | solution.py:739
